TPU v7x, 32 devices: a whole 2x2x4 slice. The times are simulated.
32 devices in a mesh: batch: 4 (over x, core), ctx: 8 (over z, y).
Axes of the slice: x: 2, y: 2, z: 4, core: 2. Of those that a mesh axis runs over, the one named last changes fastest.
Arguments:
- hidden_in: bfloat16 [4096, 1536], P(('batch', 'ctx')), may hold values from -6 to 6
- positions: int32 [4096], P(('batch', 'ctx')), may hold values from 0 to 1023, as said below
- doc_ids: int32 [4096], P(('batch', 'ctx')), may hold values from 0 to 2, as said below
- attn_gain: bfloat16 [1536], P(('batch', 'ctx')), may hold values from 0.25 to 1.75
- q_weight: bfloat16 [1536, 1536], P(('batch', 'ctx')), may hold values from -0.15625 to 0.15625
- q_bias: bfloat16 [1536], P(('batch', 'ctx')), may hold values from -3 to 3
- k_weight: bfloat16 [1536, 256], P(('batch', 'ctx')), may hold values from -0.15625 to 0.15625
- k_bias: bfloat16 [256], P(('batch', 'ctx')), may hold values from -3 to 3
- v_weight: bfloat16 [1536, 256], P(('batch', 'ctx')), may hold values from -0.15625 to 0.15625
- v_bias: bfloat16 [256], P(('batch', 'ctx')), may hold values from -3 to 3
- o_weight: bfloat16 [1536, 1536], P(('batch', 'ctx')), may hold values from -1.25 to 1.25
- mlp_gain: bfloat16 [1536], P(('batch', 'ctx')), may hold values from 0.25 to 1.75
- gate_weight: bfloat16 [1536, 8960], P(('batch', 'ctx')), may hold values from -0.15625 to 0.15625
- up_weight: bfloat16 [1536, 8960], P(('batch', 'ctx')), may hold values from -0.15625 to 0.15625
- down_weight: bfloat16 [8960, 1536], P(('batch', 'ctx')), may hold values from -0.0625 to 0.0625
- out_grad: bfloat16 [4096, 1536], P(('batch', 'ctx')), may hold values from -6 to 6
Outputs:
- hidden_out: bfloat16 [4096, 1536], P(('batch', 'ctx'))
- hidden_grad: float32 [4096, 1536], P(('batch', 'ctx'))
- attn_gain_grad: float32 [1536], P(('batch', 'ctx'))
- q_weight_grad: float32 [1536, 1536], P(('batch', 'ctx'))
- q_bias_grad: float32 [1536], P(('batch', 'ctx'))
- k_weight_grad: float32 [1536, 256], P(('batch', 'ctx'))
- k_bias_grad: float32 [256], P(('batch', 'ctx'))
- v_weight_grad: float32 [1536, 256], P(('batch', 'ctx'))
- v_bias_grad: float32 [256], P(('batch', 'ctx'))
- o_weight_grad: float32 [1536, 1536], P(('batch', 'ctx'))
- mlp_gain_grad: float32 [1536], P(('batch', 'ctx'))
- gate_weight_grad: float32 [1536, 8960], P(('batch', 'ctx'))
- up_weight_grad: float32 [1536, 8960], P(('batch', 'ctx'))
- down_weight_grad: float32 [8960, 1536], P(('batch', 'ctx'))
Inputs may be any that keep to these rules, and one draw needn't show every extreme that they name: Each device's 128 rows are 1 runs of 128 rows, run s holding tokens of sequence s of its batch index; within a batch index every position of each sequence is held exactly once. On ctx index c a run holds either positions c * 128 onward in order, or block c and then block 15 - c of 64 positions each, in order. `doc_ids`: never falls as the position within a sequence rises; each of a sequence's three documents holds 128 positions or more.
All inputs are finite; a program needn't handle non-finite values.
Results may differ from a plain program's by a relative error of at most 0.015.
Values may be sent and summed in bfloat16 or wider, within the bound.
A program may use at most 448 MiB of HBM per device.

v0:
```python
import functools
import math

import jax
import jax.numpy as jnp
from jax import lax
from jax.experimental import pallas as pl
from jax.experimental.pallas import tpu as pltpu
from jax.sharding import PartitionSpec as P

HEADS = 12
KV_HEADS = 2
GROUPS = HEADS // KV_HEADS
HEAD_DIM = 128
KVW = KV_HEADS * HEAD_DIM
INV_ROOT = HEAD_DIM ** (-0.5)
EPSILON = 1e-06
ROPE_BASE = 10000.0
MASKED = -1e30
ALL = ("batch", "ctx")
F32 = jnp.float32
BF16 = jnp.bfloat16
MESH = pl.DeviceIdType.MESH
ANYWHERE = pl.BlockSpec(memory_space=pl.ANY)
IN_VMEM = pl.BlockSpec(memory_space=pltpu.VMEM)
DMA = pltpu.SemaphoreType.DMA


def rope_tables(positions):
    half_dim = HEAD_DIM // 2
    inverse_freq = jnp.exp(
        jnp.arange(half_dim, dtype=F32) * (-2.0 * math.log(ROPE_BASE) / HEAD_DIM)
    )
    angles = positions.astype(F32)[:, None] * inverse_freq[None, :]
    angles = jnp.concatenate([angles, angles], axis=1)
    return (jnp.cos(angles), jnp.sin(angles))


def dot(lhs, rhs):
    return jnp.dot(lhs, rhs, preferred_element_type=F32)


def contract_rows(lhs, rhs):
    return lax.dot_general(lhs, rhs, (((0,), (0,)), ((), ())), preferred_element_type=F32)


def times_transposed(lhs, rhs):
    return lax.dot_general(lhs, rhs, (((1,), (1,)), ((), ())), preferred_element_type=F32)


def lanes(width):
    return -(-width // 128) * 128


def greet(devices):
    barrier = pltpu.get_barrier_semaphore()
    for device in devices:
        pl.semaphore_signal(barrier, inc=1, device_id=device, device_id_type=MESH)
    pl.semaphore_wait(barrier, len(devices))


def remote(source, target, send, receive, device):
    return pltpu.make_async_remote_copy(
        src_ref=source,
        dst_ref=target,
        send_sem=send,
        recv_sem=receive,
        device_id=device,
        device_id_type=MESH,
    )


def lasting(microseconds):
    return pl.CostEstimate(flops=0, bytes_accessed=int(3.3e6 * microseconds), transcendentals=0)


def gather_kernel(line_len, own, out, own_sem, line_sems, pair_sems):
    b, c = lax.axis_index("batch"), lax.axis_index("ctx")
    line, pair = c // 2, c % 2
    ahead = (b, 2 * lax.rem(line + 1, line_len) + pair)
    behind = (b, 2 * lax.rem(line + line_len - 1, line_len) + pair)
    across = (b, c ^ 1)
    greet((ahead, behind, across))
    keep = pltpu.make_async_copy(own, out.at[c], own_sem)
    keep.start()
    on_line, on_pair = [], []
    for step in range(line_len):
        at = 2 * lax.rem(line - step + line_len, line_len) + pair
        block = own if step == 0 else out.at[at]
        if step > 0:
            on_line[step - 1].wait_recv()
        if step < line_len - 1:
            copy = remote(block, out.at[at], line_sems.at[0, step], line_sems.at[1, step], ahead)
            copy.start()
            on_line.append(copy)
        copy = remote(block, out.at[at], pair_sems.at[0, step], pair_sems.at[1, step], across)
        copy.start()
        on_pair.append(copy)
    for copy in on_pair:
        copy.wait()
    for copy in on_line:
        copy.wait_send()
    keep.wait()


def gather_ctx(block, collective_id, name):
    n_ctx = lax.axis_size("ctx")
    line_len = n_ctx // 2
    return pl.pallas_call(
        functools.partial(gather_kernel, line_len),
        out_shape=jax.ShapeDtypeStruct((n_ctx,) + block.shape, block.dtype),
        in_specs=[ANYWHERE],
        out_specs=ANYWHERE,
        scratch_shapes=[DMA(()), DMA((2, line_len)), DMA((2, line_len))],
        compiler_params=pltpu.CompilerParams(collective_id=collective_id, has_side_effects=True),
        cost_estimate=lasting(20),
        name=name,
    )(block)


def scatter_kernel(line_len, many, *refs):
    parts, outs = refs[:many], refs[many : 2 * many]
    pair_in, line_in, line_out = (refs[(2 + i) * many : (3 + i) * many] for i in range(3))
    pair_sems, line_sems = refs[5 * many :]
    b, c = lax.axis_index("batch"), lax.axis_index("ctx")
    line, pair = c // 2, c % 2
    ahead = (b, 2 * lax.rem(line + 1, line_len) + pair)
    behind = (b, 2 * lax.rem(line + line_len - 1, line_len) + pair)
    across = (b, c ^ 1)
    greet((ahead, behind, across))

    def to(step):
        return 2 * lax.rem(line - 1 - step + line_len, line_len)

    sent, given = [], []
    for i in range(many):
        for step in range(line_len):
            copy = remote(
                parts[i].at[to(step) + 1 - pair],
                pair_in[i].at[step],
                pair_sems.at[0, i, step],
                pair_sems.at[1, i, step],
                across,
            )
            copy.start()
            given.append(copy)
    for i in range(many):
        for step in range(line_len):
            given[i * line_len + step].wait_recv()
            total = parts[i][to(step) + pair].astype(F32) + pair_in[i][step].astype(F32)
            if step > 0:
                passed.wait_recv()
                total = total + line_in[i][step - 1].astype(F32)
            if step < line_len - 1:
                line_out[i][step] = total.astype(BF16)
                passed = remote(
                    line_out[i].at[step],
                    line_in[i].at[step],
                    line_sems.at[0, i, step],
                    line_sems.at[1, i, step],
                    ahead,
                )
                passed.start()
                sent.append(passed)
            else:
                outs[i][...] = total
    for copy in given + sent:
        copy.wait_send()


def scatter_ctx(parts, collective_id, name):
    n_ctx = lax.axis_size("ctx")
    line_len, many = n_ctx // 2, len(parts)
    blocks = [(part.shape[0] // n_ctx,) + part.shape[1:] for part in parts]

    def room(size):
        return [pltpu.VMEM((size,) + block, BF16) for block in blocks]

    return pl.pallas_call(
        functools.partial(scatter_kernel, line_len, many),
        out_shape=[jax.ShapeDtypeStruct(block, F32) for block in blocks],
        in_specs=[IN_VMEM] * many,
        out_specs=[IN_VMEM] * many,
        scratch_shapes=[
            *room(line_len),
            *room(line_len - 1),
            *room(line_len - 1),
            DMA((2, many, line_len)),
            DMA((2, many, line_len)),
        ],
        compiler_params=pltpu.CompilerParams(
            collective_id=collective_id, has_side_effects=True, vmem_limit_bytes=60 * 2**20
        ),
        cost_estimate=lasting(40),
        name=name,
    )(*[part.reshape((n_ctx,) + block) for part, block in zip(parts, blocks)])


def spread_kernel(
    line_len, q_weight, k_weight, v_weight, o_weight, small, gate, up, out, columns_out, own,
    columns, own_sem, line_sems, pair_sems, chip_sems, core_sems, column_sems,
):
    b, c = lax.axis_index("batch"), lax.axis_index("ctx")
    n_ctx = 2 * line_len
    line, pair = c // 2, c % 2
    ahead = (b, 2 * lax.rem(line + 1, line_len) + pair)
    across, chip, core = (b, c ^ 1), (b ^ 2, c), (b ^ 1, c)
    others = [(b, lax.rem(c + k, n_ctx)) for k in range(1, n_ctx)]
    at = 0
    for part in (q_weight, k_weight, v_weight, o_weight, small):
        own[:, at : at + part.shape[1]] = part[...]
        at += part.shape[1]
    greet([chip, core] + others)
    keep = [pltpu.make_async_copy(own, out.at[b, c], own_sem.at[0])]
    keep[0].start()

    def pack():
        n_batch, half = out.shape[0], columns.shape[2] // 2
        piece = gate.shape[1] // (n_batch * n_ctx)
        for first, weight in ((0, gate), (half, up)):
            if n_batch * piece < half:
                columns[:, :, first + half - 128 : first + half] = jnp.zeros(
                    (n_ctx, columns.shape[1], 128), BF16
                )
            for k in range(n_batch):
                for i in range(n_ctx):
                    to = (k * n_ctx + i) * piece
                    at = first + k * piece
                    columns[i, :, at : at + piece] = weight[:, to : to + piece]
        keep.append(pltpu.make_async_copy(columns.at[c], columns_out.at[c], own_sem.at[1]))
        keep[1].start()

    def place(step, side):
        return 2 * lax.rem(line - step + line_len, line_len) + side

    def hand(block, to_b, to_c, sems, index, device):
        copy = remote(block, out.at[to_b, to_c], sems.at[0, index], sems.at[1, index], device)
        copy.start()
        return copy

    on_line, on_pair, on_chip, on_core, on_columns = [], [], [], [], []
    for step in range(line_len):
        at = place(step, pair)
        block = own if step == 0 else out.at[b, at]
        if step > 0:
            on_line[step - 1].wait_recv()
        if step < line_len - 1:
            on_line.append(hand(block, b, at, line_sems, step, ahead))
        on_pair.append(hand(block, b, at, pair_sems, step, across))
        on_chip.append(hand(block, b, at, chip_sems, step, chip))
        on_core.append(hand(block, b, at, core_sems, step, core))
        if step == 0:
            pack()
    for k, device in enumerate(others):
        copy = remote(
            columns.at[device[1]],
            columns_out.at[c],
            column_sems.at[0, k],
            column_sems.at[1, k],
            device,
        )
        copy.start()
        on_columns.append(copy)
    for step in range(line_len):
        at = place(step, 1 - pair)
        on_pair[step].wait_recv()
        on_chip.append(hand(out.at[b, at], b, at, chip_sems, line_len + step, chip))
        on_core.append(hand(out.at[b, at], b, at, core_sems, line_len + step, core))
    for index in range(n_ctx):
        at = place(index % line_len, pair if index < line_len else 1 - pair)
        on_chip[index].wait_recv()
        on_core.append(hand(out.at[b ^ 2, at], b ^ 2, at, core_sems, n_ctx + index, core))
    for copy in on_core + on_columns:
        copy.wait()
    for copy in on_line + on_pair + on_chip:
        copy.wait_send()
    for copy in keep:
        copy.wait()


def spread(matrices, gate, up, collective_id, name):
    n_batch, n_ctx = lax.axis_size("batch"), lax.axis_size("ctx")
    line_len = n_ctx // 2
    rows = gate.shape[0]
    own = (rows, sum(matrix.shape[1] for matrix in matrices))
    columns = (n_ctx, rows, 2 * lanes(gate.shape[1] // n_ctx))
    return pl.pallas_call(
        functools.partial(spread_kernel, line_len),
        out_shape=(
            jax.ShapeDtypeStruct((n_batch, n_ctx) + own, BF16),
            jax.ShapeDtypeStruct(columns, BF16),
        ),
        in_specs=[IN_VMEM] * 7,
        out_specs=(ANYWHERE, ANYWHERE),
        scratch_shapes=[
            pltpu.VMEM(own, BF16),
            pltpu.VMEM(columns, BF16),
            DMA((2,)),
            DMA((2, line_len)),
            DMA((2, line_len)),
            DMA((2, n_ctx)),
            DMA((2, 2 * n_ctx)),
            DMA((2, n_ctx)),
        ],
        compiler_params=pltpu.CompilerParams(
            collective_id=collective_id, has_side_effects=True, vmem_limit_bytes=40 * 2**20
        ),
        cost_estimate=lasting(75),
        name=name,
    )(*matrices, gate, up)


def collect_kernel(line_len, *refs):
    grads, (sums_in, columns) = refs[:2], refs[2:4]
    outs, (sums_out, columns_out) = refs[4:6], refs[6:8]
    core_in, chip_in, pair_in, line_in, chip_out, pair_out, line_out = [
        refs[8 + 2 * i : 10 + 2 * i] for i in range(7)
    ]
    sums_got, sums_mine, own_sem = refs[22:25]
    core_sems, chip_sems, pair_sems, line_sems, column_sems, sums_sems = refs[25:]
    b, c = lax.axis_index("batch"), lax.axis_index("ctx")
    n_ctx = 2 * line_len
    line, pair = c // 2, c % 2
    ahead = (b, 2 * lax.rem(line + 1, line_len) + pair)
    across, chip, core = (b, c ^ 1), (b ^ 2, c), (b ^ 1, c)
    others = [(b, lax.rem(c + k, n_ctx)) for k in range(1, n_ctx)]
    on_same_line = others[1::2]
    greet([chip, core] + others)
    keep = pltpu.make_async_copy(columns.at[c], columns_out.at[c], own_sem)
    keep.start()

    def place(index):
        step, side = index // 2, index % 2
        to = lax.rem(line - 1 - step + line_len, line_len)
        return 2 * to + (1 - pair if side == 0 else pair)

    waits = []

    def send(block, target, sems, index, device):
        copy = remote(block, target, sems.at[0, index], sems.at[1, index], device)
        copy.start()
        waits.append(copy)
        return copy

    def start_sums(index, device):
        copy = remote(
            sums_mine, sums_got.at[index], sums_sems.at[0, index], sums_sems.at[1, index], device
        )
        copy.start()
        return copy

    def add_sums(index, copy):
        copy.wait()
        sums_mine[...] += sums_got[index]

    sums_mine[...] = sums_in[...]
    by_core = start_sums(0, core)
    to_core = [[], []]
    for index in range(2 * n_ctx):
        row = b ^ 3 if index < n_ctx else b ^ 1
        for i in range(2):
            to_core[i].append(
                send(
                    grads[i].at[row, place(index % n_ctx)],
                    core_in[i].at[index],
                    core_sems.at[i],
                    index,
                    core,
                )
            )
    add_sums(0, by_core)
    by_chip = start_sums(1, chip)
    on_columns = []
    for k, device in enumerate(others):
        copy = remote(
            columns.at[device[1]],
            columns_out.at[c],
            column_sems.at[0, k],
            column_sems.at[1, k],
            device,
        )
        copy.start()
        on_columns.append(copy)
    to_chip = [[], []]
    for index in range(n_ctx):
        for i in range(2):
            to_core[i][index].wait_recv()
            total = grads[i][b ^ 2, place(index)].astype(F32) + core_in[i][index].astype(F32)
            chip_out[i][index] = total.astype(BF16)
            to_chip[i].append(
                send(chip_out[i].at[index], chip_in[i].at[index], chip_sems.at[i], index, chip)
            )
    add_sums(1, by_chip)
    by_pair = start_sums(2, across)

    def mine(i, index):
        to_core[i][n_ctx + index].wait_recv()
        to_chip[i][index].wait_recv()
        return (
            grads[i][b, place(index)].astype(F32)
            + core_in[i][n_ctx + index].astype(F32)
            + chip_in[i][index].astype(F32)
        )

    to_pair, to_line = [[], []], [[], []]
    for step in range(line_len):
        for i in range(2):
            pair_out[i][step] = mine(i, 2 * step).astype(BF16)
            to_pair[i].append(
                send(pair_out[i].at[step], pair_in[i].at[step], pair_sems.at[i], step, across)
            )
        if step == 0:
            add_sums(2, by_pair)
            own_sums = [
                send(sums_mine, sums_got.at[3 + k], sums_sems, 3 + k, device)
                for k, device in enumerate(on_same_line)
            ]
        for i in range(2):
            total = mine(i, 2 * step + 1)
            to_pair[i][step].wait_recv()
            total = total + pair_in[i][step].astype(F32)
            if step > 0:
                to_line[i][step - 1].wait_recv()
                total = total + line_in[i][step - 1].astype(F32)
            if step < line_len - 1:
                line_out[i][step] = total.astype(BF16)
                to_line[i].append(
                    send(line_out[i].at[step], line_in[i].at[step], line_sems.at[i], step, ahead)
                )
            else:
                outs[i][...] = total
    total = sums_mine[...]
    for k, copy in enumerate(own_sums):
        copy.wait_recv()
        total = total + sums_got[3 + k]
    sums_out[...] = total
    for copy in on_columns:
        copy.wait()
    for copy in waits:
        copy.wait_send()
    keep.wait()


def collect(grads, sums, columns, collective_id, name):
    n_batch, n_ctx = lax.axis_size("batch"), lax.axis_size("ctx")
    line_len = n_ctx // 2
    blocks = [grad.shape[2:] for grad in grads]

    def room(size):
        return [pltpu.VMEM((size,) + block, BF16) for block in blocks]

    return pl.pallas_call(
        functools.partial(collect_kernel, line_len),
        out_shape=(
            *[jax.ShapeDtypeStruct(block, F32) for block in blocks],
            jax.ShapeDtypeStruct(sums.shape, F32),
            jax.ShapeDtypeStruct(columns.shape, BF16),
        ),
        in_specs=[IN_VMEM] * 3 + [ANYWHERE],
        out_specs=(IN_VMEM,) * 3 + (ANYWHERE,),
        scratch_shapes=[
            *room(2 * n_ctx),
            *room(n_ctx),
            *room(line_len),
            *room(line_len - 1),
            *room(n_ctx),
            *room(line_len),
            *room(line_len - 1),
            pltpu.VMEM((2 + line_len,) + sums.shape, F32),
            pltpu.VMEM(sums.shape, F32),
            DMA(()),
            DMA((2, 2, 2 * n_ctx)),
            DMA((2, 2, n_ctx)),
            DMA((2, 2, line_len)),
            DMA((2, 2, line_len)),
            DMA((2, n_ctx)),
            DMA((2, 2 + line_len)),
        ],
        compiler_params=pltpu.CompilerParams(
            collective_id=collective_id, has_side_effects=True, vmem_limit_bytes=60 * 2**20
        ),
        cost_estimate=lasting(70),
        name=name,
    )(*grads, sums, columns)


def row_scale(values):
    return lax.rsqrt(jnp.mean(values * values, axis=-1, keepdims=True) + EPSILON)


def turn_head(values, cosine, signed_sine, back=False):
    turned = pltpu.roll(values, HEAD_DIM // 2, 1) * signed_sine
    return values * cosine - turned if back else values * cosine + turned


def whole(*shape):
    return pl.BlockSpec(shape, lambda j: (0,) * len(shape))


def project_kernel(hidden, gain, weight, bias, cosine, signed_sine, normed, query, key_value, kept):
    j = pl.program_id(0)

    @pl.when(j == 0)
    def _():
        values = hidden[...].astype(F32)
        kept[...] = (values * row_scale(values) * gain[...]).astype(BF16)
        normed[...] = kept[...]

    lin = dot(kept[...], weight[...]) + bias[...]
    tables = cosine[...], signed_sine[...]
    heads = [lin[:, i * HEAD_DIM : (i + 1) * HEAD_DIM] for i in range(4)]

    @pl.when(j < 3)
    def _():
        for i in range(4):
            turned = turn_head(heads[i], *tables)
            query[:, i * HEAD_DIM : (i + 1) * HEAD_DIM] = turned.astype(BF16)

    @pl.when(j == 3)
    def _():
        for i in range(4):
            value = turn_head(heads[i], *tables) if i < KV_HEADS else heads[i]
            key_value[:, i * HEAD_DIM : (i + 1) * HEAD_DIM] = value.astype(BF16)


def project(hidden, gain, weights, bias, tables):
    count, width = hidden.shape
    wide = 2 * KVW
    table = whole(count, HEAD_DIM)
    return pl.pallas_call(
        project_kernel,
        grid=(4,),
        out_shape=(
            jax.ShapeDtypeStruct((count, width), BF16),
            jax.ShapeDtypeStruct((count, width), BF16),
            jax.ShapeDtypeStruct((count, wide), BF16),
        ),
        in_specs=[
            whole(count, width),
            whole(1, width),
            pl.BlockSpec((width, wide), lambda j: (0, j)),
            pl.BlockSpec((1, wide), lambda j: (0, j)),
            table,
            table,
        ],
        out_specs=(
            whole(count, width),
            pl.BlockSpec((count, wide), lambda j: (0, jnp.minimum(j, 2))),
            whole(count, wide),
        ),
        scratch_shapes=[pltpu.VMEM((count, width), BF16)],
        compiler_params=pltpu.CompilerParams(vmem_limit_bytes=40 * 2**20),
        cost_estimate=lasting(4),
        name="project",
    )(hidden, gain, weights, bias, *tables)


def mark_allowed(key_pos, key_doc, own_pos, own_doc, allowed):
    count = own_pos.shape[1]
    pos_column, doc_column = key_pos[...].T, key_doc[...].T
    for i in range(key_pos.shape[0]):
        seen = (pos_column[:, i : i + 1] <= own_pos[...]) & (doc_column[:, i : i + 1] == own_doc[...])
        allowed[i * count : (i + 1) * count] = jnp.where(seen, 1.0, 0.0)


def stack_heads(block, group):
    return jnp.concatenate(
        [block[:, i * HEAD_DIM : (i + 1) * HEAD_DIM] for i in range(group)], axis=0
    )


def lay_heads(stacked, group):
    count = stacked.shape[0] // group
    return jnp.concatenate([stacked[i * count : (i + 1) * count] for i in range(group)], axis=1)


def probabilities(keys, queries, allowed, group):
    scores = times_transposed(keys, queries) * INV_ROOT
    seen = jnp.concatenate([allowed[...]] * group, axis=1) > 0.0
    scores = jnp.where(seen, scores, MASKED)
    raised = jnp.exp(scores - jnp.max(scores, axis=0, keepdims=True))
    return raised * (1.0 / jnp.sum(raised, axis=0, keepdims=True))


def attend_kernel(
    group, last, query, keys, values, out_0, out_1, out_2, key_pos, key_doc, own_pos, own_doc,
    hidden, gain, attn_out, residual, normed, total, allowed,
):
    j = pl.program_id(0)

    @pl.when(j == 0)
    def _():
        total[...] = hidden[...].astype(F32)
        mark_allowed(key_pos, key_doc, own_pos, own_doc, allowed)

    probs = probabilities(keys[...], stack_heads(query[...], group), allowed, group)
    result = contract_rows(values[...], probs.astype(BF16)).T
    block = lay_heads(result, group).astype(BF16)
    attn_out[...] = block
    for t, weight in enumerate((out_0, out_1, out_2)):
        total[:, t * 512 : (t + 1) * 512] += dot(block, weight[...])

    @pl.when(j == last)
    def _():
        values = total[...]
        residual[...] = values
        normed[...] = (values * row_scale(values) * gain[...]).astype(BF16)


def head_specs(count, width, keys, group, weights_at):
    rows = group * HEAD_DIM
    per_key = GROUPS // group
    query = pl.BlockSpec((count, rows), lambda j: (0, j))
    heads = [
        pl.BlockSpec((keys, HEAD_DIM), lambda j, i=i: (0, KV_HEADS * i + j // per_key))
        for i in range(2)
    ]
    out = [
        pl.BlockSpec((rows, 512), lambda j, t=t: (j, weights_at // 512 + t))
        for t in range(width // 512)
    ]
    places = [whole(keys // count, count)] * 2 + [whole(1, count)] * 2
    return query, heads, out, places


def attend(query, key_value, weights, places, hidden, gain):
    count, width = hidden.shape
    keys = key_value.shape[0]
    group = 3 if keys <= 1024 else 1
    steps = HEADS // group
    query_spec, head_spec, out_spec, place_spec = head_specs(
        count, width, keys, group, width + 2 * KVW
    )
    return pl.pallas_call(
        functools.partial(attend_kernel, group, steps - 1),
        grid=(steps,),
        out_shape=(
            jax.ShapeDtypeStruct((count, width), BF16),
            jax.ShapeDtypeStruct((count, width), F32),
            jax.ShapeDtypeStruct((count, width), BF16),
        ),
        in_specs=[query_spec, *head_spec, *out_spec, *place_spec]
        + [whole(count, width), whole(1, width)],
        out_specs=(query_spec, whole(count, width), whole(count, width)),
        scratch_shapes=[pltpu.VMEM((count, width), F32), pltpu.VMEM((keys, count), F32)],
        compiler_params=pltpu.CompilerParams(vmem_limit_bytes=56 * 2**20),
        cost_estimate=lasting(10),
        name="attend",
    )(query, key_value, key_value, *[weights] * 3, *places, hidden, gain)


def attend_back_kernel(
    group, per_key, query, keys, values, out_0, out_1, out_2, key_pos, key_doc, own_pos, own_doc,
    attn_out, residual, gain, out_grad, d_normed, cosine, signed_sine, d_query, d_key_value,
    o_grad, d_residual, gain_grad, branch, allowed, key_sum, value_sum,
):
    j = pl.program_id(0)

    @pl.when(j == 0)
    def _():
        rows, grads = residual[...], d_normed[...]
        factor = row_scale(rows)
        scaled = grads * gain[...]
        gain_grad[...] = jnp.sum(grads * rows * factor, axis=0, keepdims=True)
        total = out_grad[...].astype(F32) + (
            factor * scaled
            - rows * (factor * factor * factor) * jnp.mean(scaled * rows, axis=-1, keepdims=True)
        )
        d_residual[...] = total
        branch[...] = total.astype(BF16)
        mark_allowed(key_pos, key_doc, own_pos, own_doc, allowed)

    @pl.when(lax.rem(j, per_key) == 0)
    def _():
        key_sum[...] = jnp.zeros_like(key_sum)
        value_sum[...] = jnp.zeros_like(value_sum)

    o_grad[...] = contract_rows(attn_out[...], branch[...]).astype(BF16)
    d_attn = sum(
        times_transposed(branch[:, t * 512 : (t + 1) * 512], weight[...])
        for t, weight in enumerate((out_0, out_1, out_2))
    ).astype(BF16)
    grads = stack_heads(d_attn, group)
    queries = stack_heads(query[...], group)
    probs = probabilities(keys[...], queries, allowed, group)
    d_probs = times_transposed(values[...], grads)
    delta = jnp.sum(probs * d_probs, axis=0, keepdims=True)
    d_scores = (probs * (d_probs - delta)).astype(BF16)
    key_sum[...] += dot(d_scores, queries)
    value_sum[...] += dot(probs.astype(BF16), grads)
    result = contract_rows(keys[...], d_scores).T * INV_ROOT
    count = result.shape[0] // group
    for i in range(group):
        head = turn_head(
            result[i * count : (i + 1) * count], cosine[...], signed_sine[...], back=True
        )
        d_query[:, i * HEAD_DIM : (i + 1) * HEAD_DIM] = head.astype(BF16)

    @pl.when(lax.rem(j, per_key) == per_key - 1)
    def _():
        at = pl.multiple_of(j // per_key * HEAD_DIM, HEAD_DIM)
        d_key_value[:, pl.ds(at, HEAD_DIM)] = (key_sum[...] * INV_ROOT).astype(BF16)
        d_key_value[:, pl.ds(KVW + at, HEAD_DIM)] = value_sum[...].astype(BF16)


def attend_back(query, key_value, weights, places, attn_out, residual, gain, out_grad, d_normed, tables):
    count, width = query.shape
    keys = key_value.shape[0]
    group = 3 if keys <= 1024 else 1
    steps = HEADS // group
    query_spec, head_spec, out_spec, place_spec = head_specs(
        count, width, keys, group, width + 2 * KVW
    )
    rows, table = whole(count, width), whole(count, HEAD_DIM)
    return pl.pallas_call(
        functools.partial(attend_back_kernel, group, GROUPS // group),
        grid=(steps,),
        out_shape=(
            jax.ShapeDtypeStruct((count, width), BF16),
            jax.ShapeDtypeStruct((keys, 2 * KVW), BF16),
            jax.ShapeDtypeStruct((width, width), BF16),
            jax.ShapeDtypeStruct((count, width), F32),
            jax.ShapeDtypeStruct((1, width), F32),
        ),
        in_specs=[query_spec, *head_spec, *out_spec, *place_spec, query_spec]
        + [rows, whole(1, width), rows, rows, table, table],
        out_specs=(
            query_spec,
            whole(keys, 2 * KVW),
            pl.BlockSpec((group * HEAD_DIM, width), lambda j: (j, 0)),
            rows,
            whole(1, width),
        ),
        scratch_shapes=[
            pltpu.VMEM((count, width), BF16),
            pltpu.VMEM((keys, count), F32),
            pltpu.VMEM((keys, HEAD_DIM), F32),
            pltpu.VMEM((keys, HEAD_DIM), F32),
        ],
        compiler_params=pltpu.CompilerParams(vmem_limit_bytes=60 * 2**20),
        cost_estimate=lasting(17),
        name="attend_back",
    )(
        query, key_value, key_value, *[weights] * 3, *places, attn_out, residual, gain, out_grad,
        d_normed, *tables,
    )


def project_back_kernel(
    d_query, d_key_value, weight, normed, hidden, gain, d_residual, gain_two_grad, cosine,
    signed_sine, grad, hidden_grad, sums, flipped, total, biases,
):
    j = pl.program_id(0)
    wide = weight.shape[1]

    @pl.when(j == 0)
    def _():
        flipped[...] = normed[...].astype(F32).T.astype(BF16)
        total[...] = jnp.zeros_like(total)
        sums[...] = jnp.zeros_like(sums)

    def add(d_lin):
        grad[...] = dot(flipped[...], d_lin).astype(BF16)
        total[...] += times_transposed(d_lin, weight[...])
        return jnp.sum(d_lin.astype(F32), axis=0, keepdims=True)

    for i in range(3):

        @pl.when(j == i)
        def _():
            sums[1:2, i * wide : (i + 1) * wide] = add(d_query[...])

    @pl.when(j == 3)
    def _():
        heads = [
            turn_head(
                d_key_value[:, i * HEAD_DIM : (i + 1) * HEAD_DIM],
                cosine[...],
                signed_sine[...],
                back=True,
            )
            for i in range(KV_HEADS)
        ]
        d_lin = jnp.concatenate(heads + [d_key_value[:, KVW:]], axis=1).astype(BF16)
        sums[2:3, :wide] = add(d_lin)
        rows, grads = hidden[...].astype(F32), total[...]
        factor = row_scale(rows)
        scaled = grads * gain[...]
        sums[0:1] = jnp.sum(grads * rows * factor, axis=0, keepdims=True)
        sums[3:4] = gain_two_grad[...]
        hidden_grad[...] = d_residual[...] + (
            factor * scaled
            - rows * (factor * factor * factor) * jnp.mean(scaled * rows, axis=-1, keepdims=True)
        )


def project_back(d_query, d_key_value, weights, normed, hidden, gain, d_residual, gain_two_grad, tables):
    count, width = hidden.shape
    wide = 2 * KVW
    rows, table = whole(count, width), whole(count, HEAD_DIM)
    return pl.pallas_call(
        project_back_kernel,
        grid=(4,),
        out_shape=(
            jax.ShapeDtypeStruct((width, width + wide), BF16),
            jax.ShapeDtypeStruct((count, width), F32),
            jax.ShapeDtypeStruct((8, width), F32),
        ),
        in_specs=[
            pl.BlockSpec((count, wide), lambda j: (0, jnp.minimum(j, 2))),
            whole(count, wide),
            pl.BlockSpec((width, wide), lambda j: (0, j)),
            rows,
            rows,
            whole(1, width),
            rows,
            whole(1, width),
            table,
            table,
        ],
        out_specs=(
            pl.BlockSpec((width, wide), lambda j: (0, j)),
            rows,
            whole(8, width),
        ),
        scratch_shapes=[
            pltpu.VMEM((width, count), BF16),
            pltpu.VMEM((count, width), F32),
            pltpu.VMEM((8, wide), F32),
        ],
        compiler_params=pltpu.CompilerParams(vmem_limit_bytes=48 * 2**20),
        cost_estimate=lasting(9),
        name="project_back",
    )(
        d_query, d_key_value, weights, normed, hidden, gain, d_residual, gain_two_grad, *tables
    )


def unpack_kernel(n_batch, piece, packed, gate, up):
    n_ctx, _, both = packed.shape
    for out, first in ((gate, 0), (up, both // 2)):
        for k in range(n_batch):
            for i in range(n_ctx):
                at = first + k * piece
                to = (k * n_ctx + i) * piece
                out[:, to : to + piece] = packed[i, :, at : at + piece].astype(F32)


def unpack(packed, n_batch, width):
    n_ctx, rows, _ = packed.shape
    out = jax.ShapeDtypeStruct((rows, width), F32)
    return pl.pallas_call(
        functools.partial(unpack_kernel, n_batch, width // (n_batch * n_ctx)),
        out_shape=(out, out),
        in_specs=[IN_VMEM],
        out_specs=(IN_VMEM, IN_VMEM),
        compiler_params=pltpu.CompilerParams(vmem_limit_bytes=40 * 2**20),
        cost_estimate=lasting(3),
        name="unpack",
    )(packed)


def mlp_kernel(line_len, tile, own_rows, *refs):
    n_batch, n_ctx = 4, 2 * line_len
    weights, (down, grads_in) = refs[:n_batch], refs[n_batch : n_batch + 2]
    d_rows_out, ff_out, down_out, gate_up_out = refs[n_batch + 2 : n_batch + 6]
    (
        tokens, flipped, gate_up, down_in, grads, mixed, mixed_flipped, d_gate_up, d_parts, ff_parts,
        d_pair, d_line, d_pass, ff_pair, ff_line, ff_pass, core_wide, chip_wide, down_terms,
        core_down, chip_down, own, load_sems, store_sems,
        line_sems, pair_sems, back_pair, back_line, batch_sems,
    ) = refs[n_batch + 6 :]
    b, c = lax.axis_index("batch"), lax.axis_index("ctx")
    line, pair = c // 2, c % 2
    ahead = (b, 2 * lax.rem(line + 1, line_len) + pair)
    behind = (b, 2 * lax.rem(line + line_len - 1, line_len) + pair)
    across, chip, core = (b, c ^ 1), (b ^ 2, c), (b ^ 1, c)
    count, width = own.shape
    half = gate_up.shape[1] // 2
    own_ff = down.shape[0]
    piece = own_ff // n_batch
    depth = width // n_batch
    for k in range(n_batch):
        source = pl.ds(pl.multiple_of((b ^ k) * depth, 128), depth)
        own[:, k * depth : (k + 1) * depth] = own_rows[:, source]
    greet((ahead, behind, across, chip, core))

    def at(step):
        return 2 * lax.rem(line - step + line_len, line_len)

    sent = []

    def send(source, target, sems, device):
        copy = remote(source, target, sems[0], sems[1], device)
        copy.start()
        sent.append(copy)
        return copy

    on_line, on_pair = [], []

    def forward(step):
        block = own if step == 0 else tokens.at[at(step) + pair]
        target = tokens.at[at(step) + pair]
        if step > 0:
            on_line[step - 1].wait_recv()
        if step < line_len - 1:
            sems = line_sems.at[0, step], line_sems.at[1, step]
            on_line.append(send(block, target, sems, ahead))
        sems = pair_sems.at[0, step], pair_sems.at[1, step]
        on_pair.append(send(block, target, sems, across))

    forward(0)
    loads = [pltpu.make_async_copy(own, tokens.at[c], load_sems.at[0])]
    for k, weight in enumerate(weights):
        loads.append(
            pltpu.make_async_copy(
                weight, gate_up.at[pl.ds(k * depth, depth)], load_sems.at[1 + k]
            )
        )
    loads.append(
        pltpu.make_async_copy(down, down_in.at[pl.ds(0, own_ff)], load_sems.at[1 + n_batch])
    )
    loads.append(pltpu.make_async_copy(grads_in, grads, load_sems.at[2 + n_batch]))
    for copy in loads:
        copy.start()
    if own_ff < half:
        down_in[own_ff:half] = jnp.zeros((half - own_ff, width), BF16)
    for copy in loads:
        copy.wait()

    def chunk(step):
        first = pl.multiple_of(at(step) * count, 2 * count)
        rows, pair_rows = pl.ds(first, 2 * count), pl.ds(at(step), 2)
        block = tokens[pair_rows].reshape(2 * count, width)
        grad_block = grads[pair_rows].reshape(2 * count, width)

        def columns(index, _):
            low = pl.multiple_of(index * tile, 128)
            high = pl.multiple_of(half + index * tile, 128)
            gate_lin = dot(block, gate_up[:, pl.ds(low, tile)])
            up_lin = dot(block, gate_up[:, pl.ds(high, tile)])
            d_mixed = times_transposed(grad_block, down_in[pl.ds(low, tile)])
            sigmoid = 1.0 / (1.0 + jnp.exp(-gate_lin))
            silu = gate_lin * sigmoid
            product = silu * up_lin
            mixed[:, pl.ds(low, tile)] = product.astype(BF16)
            mixed_flipped[pl.ds(low, tile), rows] = product.T.astype(BF16)
            d_gate = d_mixed * up_lin * sigmoid * (1.0 + gate_lin * (1.0 - sigmoid))
            d_gate_up[rows, pl.ds(low, tile)] = d_gate.astype(BF16)
            d_gate_up[rows, pl.ds(high, tile)] = (d_mixed * silu).astype(BF16)
            return 0

        lax.fori_loop(0, half // tile, columns, 0)

        def features(index, _):
            low = pl.multiple_of(index * depth, 128)
            at_low = pl.ds(low, depth)
            back = times_transposed(d_gate_up[rows], gate_up[at_low])
            d_parts[pair_rows, :, at_low] = back.astype(BF16).reshape(2, count, depth)
            return 0

        lax.fori_loop(0, n_batch, features, 0)

        def outputs(index, _):
            low = pl.multiple_of(index * depth, 128)
            at_low = pl.ds(low, depth)
            out = dot(mixed[...], down_in[:, at_low])
            ff_parts[pair_rows, :, at_low] = out.astype(BF16).reshape(2, count, depth)
            flipped[at_low, rows] = (
                tokens[pair_rows, :, at_low].reshape(2 * count, depth).astype(F32).T.astype(BF16)
            )
            return 0

        lax.fori_loop(0, n_batch, outputs, 0)

    moves = (
        (d_parts, d_pair, d_line, d_pass, d_rows_out),
        (ff_parts, ff_pair, ff_line, ff_pass, ff_out),
    )
    given = {}

    def give(index, which=0):
        parts, pairs = moves[which][:2]
        sems = back_pair.at[0, which, index], back_pair.at[1, which, index]
        source = parts.at[at(index + 1) + 1 - pair]
        given[index, which] = send(source, pairs.at[index], sems, across)

    for step in range(line_len):
        if step + 1 < line_len:
            forward(step + 1)
        on_pair[step].wait_recv()
        chunk(step)
        if step == line_len - 2:
            for index in range(line_len - 2):
                give(index)
    give(line_len - 2)
    give(line_len - 1)
    stores = []

    def store(source, target):
        copy = pltpu.make_async_copy(source, target, store_sems.at[len(stores)])
        copy.start()
        stores.append(copy)

    passed = {}

    def passing(index, which=0):
        parts, pairs, lines, passes, out = moves[which]
        given[index, which].wait_recv()
        total = parts[at(index + 1) + pair].astype(F32) + pairs[index].astype(F32)
        if index > 0:
            passed[index - 1, which].wait_recv()
            total = total + lines[index - 1].astype(F32)
        if index < line_len - 1:
            passes[index] = total.astype(BF16)
            sems = back_line.at[0, which, index], back_line.at[1, which, index]
            passed[index, which] = send(passes.at[index], lines.at[index], sems, ahead)
        elif which:
            out[...] = total
        else:
            for k in range(n_batch):
                target = pl.ds(pl.multiple_of((b ^ k) * depth, 128), depth)
                out[:, target] = total[:, k * depth : (k + 1) * depth]

    def batch_send(source, target, index, device):
        sems = batch_sems.at[0, index], batch_sems.at[1, index]
        return send(source, target, sems, device)

    def wide(k, side):
        return gate_up.at[pl.ds(k * depth, depth), pl.ds(side * half, half)]

    def weight_grad(k, side):
        def columns(index, _):
            at_low = pl.ds(pl.multiple_of(side * half + index * tile, 128), tile)
            grad = dot(flipped[k * depth : (k + 1) * depth], d_gate_up[:, at_low])
            gate_up[k * depth : (k + 1) * depth, at_low] = grad.astype(BF16)
            return 0

        lax.fori_loop(0, half // tile, columns, 0)

    def down_grads():
        for k in range(n_batch):
            grad = dot(
                mixed_flipped[k * piece : (k + 1) * piece],
                grads[...].reshape(n_ctx * count, width),
            )
            down_terms[k] = grad.astype(BF16)
        for slot, row in ((1, b ^ 3), (0, b ^ 1)):
            to_core["down", slot] = batch_send(
                down_terms.at[row], core_down.at[slot], 6 + slot, core
            )

    def pass_down():
        to_core["down", 1].wait_recv()
        total = down_terms[b ^ 2].astype(F32) + core_down[1].astype(F32)
        down_terms[b ^ 2] = total.astype(BF16)
        to_chip.append(batch_send(down_terms.at[b ^ 2], chip_down, 8, chip))

    def add_wide(k, side, terms):
        def columns(index, _):
            low = pl.multiple_of(index * tile, 128)
            at_low = pl.ds(pl.multiple_of(side * half + low, 128), tile)
            rows = slice(k * depth, (k + 1) * depth)
            total = gate_up[rows, at_low].astype(F32)
            for term in terms:
                total = total + term[:, pl.ds(low, tile)].astype(F32)
            gate_up[rows, at_low] = total.astype(BF16)
            return 0

        lax.fori_loop(0, half // tile, columns, 0)

    to_core, to_chip = {}, []

    def compute_and_send(k, side):
        weight_grad(k, side)
        slot = k // 2
        target = core_wide.at[slot, side]
        to_core[k, side] = batch_send(wide(k, side), target, 2 * slot + side, core)

    def compute_and_pass(side):
        weight_grad(2, side)
        to_core[3, side].wait_recv()
        add_wide(2, side, [core_wide.at[1, side]])
        to_chip.append(batch_send(wide(2, side), chip_wide.at[side], 4 + side, chip))

    compute_and_send(3, 0)
    compute_and_pass(0)
    compute_and_send(3, 1)
    compute_and_pass(1)
    work = [
        down_grads,
        lambda: (pass_down(), compute_and_send(1, 0)),
        lambda: compute_and_send(1, 1),
        lambda: (weight_grad(0, 0), weight_grad(0, 1)),
    ]
    for index in range(max(line_len, len(work))):
        if index < line_len:
            passing(index)
            give(index, 1)
        if index < len(work):
            work[index]()
    for index in range(line_len - 1):
        passing(index, 1)
    for side in range(2):
        to_core[1, side].wait_recv()
        to_chip[side].wait_recv()
        add_wide(0, side, [core_wide.at[0, side], chip_wide.at[side]])
        store(wide(0, side), gate_up_out.at[:, pl.ds(side * half, half)])
    to_core["down", 0].wait_recv()
    to_chip[2].wait_recv()
    down_out[...] = (
        down_terms[b].astype(F32) + core_down[0].astype(F32) + chip_down[...].astype(F32)
    )
    passing(line_len - 1, 1)
    for copy in sent:
        copy.wait_send()
    for copy in stores:
        copy.wait()


def mlp_scratch(n_ctx, n_batch, count, width, hidden_own):
    line_len, half = n_ctx // 2, lanes(hidden_own)
    tokens, piece = n_ctx * count, hidden_own // n_batch

    def room(*shape):
        return pltpu.VMEM(shape, BF16)

    return [
        room(n_ctx, count, width),
        room(width, tokens),
        room(width, 2 * half),
        room(half, width),
        room(n_ctx, count, width),
        room(2 * count, half),
        room(half, tokens),
        room(tokens, 2 * half),
        room(n_ctx, count, width),
        room(n_ctx, count, width),
        *[room(line_len, count, width), *[room(line_len - 1, count, width)] * 2] * 2,
        room(2, 2, width // n_batch, half),
        room(2, width // n_batch, half),
        room(n_batch, piece, width),
        room(2, piece, width),
        room(piece, width),
        room(count, width),
    ]


def mlp(own, weights, down, grads, collective_id, name):
    n_batch, n_ctx = lax.axis_size("batch"), lax.axis_size("ctx")
    line_len = n_ctx // 2
    count, width = own.shape
    half = weights[0].shape[1] // 2
    tile = 384 if half % 384 == 0 else 128
    return pl.pallas_call(
        functools.partial(mlp_kernel, line_len, tile),
        out_shape=(
            jax.ShapeDtypeStruct((count, width), F32),
            jax.ShapeDtypeStruct((count, width), F32),
            jax.ShapeDtypeStruct((down.shape[0] // n_batch, width), F32),
            jax.ShapeDtypeStruct(weights[0].shape, BF16),
        ),
        in_specs=[IN_VMEM] + [ANYWHERE] * (n_batch + 2),
        out_specs=(IN_VMEM, IN_VMEM, IN_VMEM, ANYWHERE),
        scratch_shapes=mlp_scratch(n_ctx, n_batch, count, width, down.shape[0])
        + [
            DMA((3 + n_batch,)),
            DMA((2,)),
            DMA((2, line_len)),
            DMA((2, line_len)),
            DMA((2, 2, line_len)),
            DMA((2, 2, line_len)),
            DMA((2, 9)),
        ],
        compiler_params=pltpu.CompilerParams(
            collective_id=collective_id, has_side_effects=True, vmem_limit_bytes=60 * 2**20
        ),
        cost_estimate=lasting(100),
        name=name,
    )(own, *weights, down, grads.reshape(n_ctx, count, width))


def front_kernel(line_len, group, *refs):
    (
        q_weight, k_weight, v_weight, o_weight, small, gate, up, hidden, cosine, signed_sine,
        own_pos, own_doc, down, out_grad,
    ) = refs[:14]
    (
        normed_out, query, attn_out, residual, normed_two, gain_one, gain_two, key_pos, key_doc,
        key_value_out, w_in_out, w_out_out, columns_out, near, far, farther, down_out, grads_out,
    ) = refs[14:32]
    own_in, w_in, w_out, columns, key_own, key_value, allowed, vectors, bias = refs[32:41]
    (
        load_sems, line_sems, first_sems, second_sems, core_sems, column_sems, near_sems, far_sems,
        farther_sems, keys_line_sems, keys_pair_sems, grads_line_sems, grads_pair_sems, down_sems,
    ) = refs[41:]
    b, c = lax.axis_index("batch"), lax.axis_index("ctx")
    n_batch, n_ctx = 4, 2 * line_len
    line, pair = c // 2, c % 2
    ahead = (b, 2 * lax.rem(line + 1, line_len) + pair)
    across, chip, core = (b, c ^ 1), (b ^ 2, c), (b ^ 1, c)
    others = [(b, lax.rem(c + k, n_ctx)) for k in range(1, n_ctx)]
    count, width = hidden.shape
    rows = q_weight.shape[0]
    wide = width + 2 * KVW
    at = 0
    for part in (q_weight, k_weight, v_weight):
        own_in[:, at : at + part.shape[1]] = part[...]
        at += part.shape[1]
    own_in[:, at:] = small[...]
    greet([chip, core] + others)
    sent, local = [], []

    def send(source, target, sems, index, device):
        copy = remote(source, target, sems.at[(0, *index)], sems.at[(1, *index)], device)
        copy.start()
        sent.append(copy)
        return copy

    def store(source, target):
        copy = pltpu.make_async_copy(source, target, load_sems.at[len(local)])
        copy.start()
        local.append(copy)

    owns, wholes = (own_in, o_weight), (w_in, w_out)
    first_to, second_to = (across, chip), (chip, across)
    on_line, on_first, on_second, on_core = {}, {}, {}, {}

    def place(step, side):
        return 2 * lax.rem(line - step + line_len, line_len) + side

    def block(p, row, column):
        first = pl.multiple_of((row * n_ctx + column) * rows, rows)
        return wholes[p].at[pl.ds(first, rows)]

    def line_step(p, step):
        target = block(p, b, place(step, pair))
        source = owns[p] if step == 0 else target
        if step > 0:
            on_line[p, step - 1].wait_recv()
        if step < line_len - 1:
            on_line[p, step] = send(source, target, line_sems, (p, step), ahead)
        on_first[p, step] = send(source, target, first_sems, (p, step), first_to[p])
        on_second[p, step] = send(source, target, second_sems, (p, step), second_to[p])
        on_core[p, step] = send(source, target, core_sems, (p, step), core)

    def first_step(p, step):
        on_first[p, step].wait_recv()
        row, side = ((b, 1 - pair), (b ^ 2, pair))[p]
        landed = block(p, row, place(step, side))
        index = line_len + step
        on_second[p, index] = send(landed, landed, second_sems, (p, index), second_to[p])
        on_core[p, index] = send(landed, landed, core_sems, (p, index), core)

    def second_step(p, index):
        on_second[p, index].wait_recv()
        late = index >= line_len
        row = b ^ 2 if p == 0 or late else b
        side = 1 - pair if p == 1 or late else pair
        landed = block(p, row, place(index % line_len, side))
        on_core[p, n_ctx + index] = send(landed, landed, core_sems, (p, n_ctx + index), core)

    def complete(p):
        for index in range(2 * n_ctx):
            on_core[p, index].wait_recv()

    on_down = []

    def down_step(step):
        if step == 0:
            store(down, down_out.at[b])
            on_down.append(send(down, down_out.at[b], down_sems, (0,), chip))
            on_down.append(send(down, down_out.at[b], down_sems, (1,), core))
        else:
            on_down[0].wait_recv()
            landed = down_out.at[b ^ 2]
            on_down.append(send(landed, landed, down_sems, (2,), core))

    def pack():
        half = columns.shape[2] // 2
        piece = gate.shape[1] // (n_batch * n_ctx)
        for first, weight in ((0, gate), (half, up)):
            if n_batch * piece < half:
                columns[:, :, first + half - 128 : first + half] = jnp.zeros(
                    (n_ctx, columns.shape[1], 128), BF16
                )
            for k in range(n_batch):
                for i in range(n_ctx):
                    to = (k * n_ctx + i) * piece
                    low = first + k * piece
                    columns[i, :, low : low + piece] = weight[:, to : to + piece]
        store(columns.at[c], columns_out.at[c])

    on_columns, on_near, on_far, on_farther = [], [], [], []

    def exchange_columns(first, last):
        for k in range(first, last):
            source = columns.at[others[k][1]]
            on_columns.append(send(source, columns_out.at[c], column_sems, (k,), others[k]))

    def spread_columns(k):
        slot = lax.rem(c - k + n_ctx, n_ctx)
        if k > 0:
            on_columns[k - 1].wait_recv()
        source = columns_out.at[slot] if k > 0 else columns.at[c]
        on_far.append(send(source, far.at[slot], far_sems, (k,), chip))
        on_near.append(send(source, near.at[slot], near_sems, (k,), core))

    def spread_farther(k):
        slot = lax.rem(c - k + n_ctx, n_ctx)
        on_far[k].wait_recv()
        on_farther.append(send(far.at[slot], farther.at[slot], farther_sems, (k,), core))

    keys_line, keys_pair = [], []

    def keys_step(step):
        column = place(step, pair)
        source = key_own if step == 0 else key_value.at[column]
        if step > 0:
            keys_line[step - 1].wait_recv()
        if step < line_len - 1:
            keys_line.append(send(source, key_value.at[column], keys_line_sems, (step,), ahead))
        keys_pair.append(send(source, key_value.at[column], keys_pair_sems, (step,), across))

    grads_line, grads_pair = [], []

    def grads_step(step):
        target = grads_out.at[place(step, pair)]
        source = out_grad if step == 0 else target
        if step > 0:
            grads_line[step - 1].wait_recv()
        if step < line_len - 1:
            grads_line.append(send(source, target, grads_line_sems, (step,), ahead))
        grads_pair.append(send(source, target, grads_pair_sems, (step,), across))

    line_step(0, 0)
    mine = pl.ds(pl.multiple_of((b * n_ctx + c) * rows, rows), rows)
    w_in[mine] = own_in[...]
    w_out[mine] = o_weight[...]
    pack()
    for step in range(1, line_len):
        line_step(0, step)
    exchange_columns(0, 2)
    line_step(1, 0)
    for step in range(line_len):
        first_step(0, step)
    between = [functools.partial(line_step, 1, step) for step in range(1, line_len)]
    between += [functools.partial(first_step, 1, step) for step in range(line_len)]
    between += [functools.partial(down_step, 0)]
    for index in range(n_ctx):
        second_step(0, index)
        between[index]()
        if index in (1, 3, 4, 5, 6):
            exchange_columns(len(on_columns), len(on_columns) + 1)
    store(out_grad, grads_out.at[c])
    complete(0)

    values = hidden[...].astype(F32)
    for d in range(n_batch * n_ctx):
        piece = w_in[d * rows : d * rows + 16, wide:].astype(F32)
        vectors[0:3, d * rows : (d + 1) * rows] = piece[0:3, :rows]
        part = KVW // (n_batch * n_ctx)
        for i in range(2):
            bias[0:1, i * KVW + d * part : i * KVW + (d + 1) * part] = piece[3 + i : 4 + i, :part]
    for k in range(n_ctx):
        first = pl.multiple_of((b * n_ctx + k) * rows, rows)
        piece = w_in[pl.ds(first, 16), wide:].astype(F32)
        key_pos[k : k + 1] = piece[5:6] * 64.0 + piece[6:7]
        key_doc[k : k + 1] = piece[7:8]
    gain_one[...] = vectors[0:1]
    gain_two[...] = vectors[1:2]
    normed_out[...] = (values * row_scale(values) * vectors[0:1]).astype(BF16)
    tables = cosine[...], signed_sine[...]
    lin = dot(normed_out[...], w_in[:, width:wide]) + bias[...]
    for i in range(2 * KV_HEADS):
        head = lin[:, i * HEAD_DIM : (i + 1) * HEAD_DIM]
        head = turn_head(head, *tables) if i < KV_HEADS else head
        key_own[:, i * HEAD_DIM : (i + 1) * HEAD_DIM] = head.astype(BF16)
    keys_step(0)
    key_value[c] = key_own[...]
    for k in range(3):
        step = width // 3
        part = slice(k * step, (k + 1) * step)
        lin = dot(normed_out[...], w_in[:, part]) + vectors[2:3, part]
        for i in range(step // HEAD_DIM):
            head = turn_head(lin[:, i * HEAD_DIM : (i + 1) * HEAD_DIM], *tables)
            low = k * step + i * HEAD_DIM
            query[:, low : low + HEAD_DIM] = head.astype(BF16)
    store(w_in, w_in_out)
    mark_allowed(key_pos, key_doc, own_pos, own_doc, allowed)
    spread_columns(0)
    for step in range(1, line_len):
        second_step(1, step - 1)
        keys_step(step)
    for step in range(line_len):
        keys_pair[step].wait_recv()
    store(key_value, key_value_out)
    grads_step(0)

    def attention(i):
        wide_part = group * HEAD_DIM
        part = slice(i * wide_part, (i + 1) * wide_part)
        head = i * group // GROUPS * HEAD_DIM
        keys = key_value[:, :, head : head + HEAD_DIM].reshape(n_ctx * count, HEAD_DIM)
        low = KVW + head
        values = key_value[:, :, low : low + HEAD_DIM].reshape(n_ctx * count, HEAD_DIM)
        probs = probabilities(keys, stack_heads(query[:, part], group), allowed, group)
        result = contract_rows(values, probs.astype(BF16)).T
        attn_out[:, part] = lay_heads(result, group).astype(BF16)

    steps = HEADS // group
    for i in range(steps):
        attention(i)
        for index in range(line_len - 1 + i, n_ctx, steps):
            second_step(1, index)
        for k in range(1 + 2 * i, min(3 + 2 * i, n_ctx)):
            spread_columns(k)
        if i == steps // 2:
            grads_step(1)
    down_step(1)
    complete(1)
    store(w_out, w_out_out)
    total = hidden[...].astype(F32) + dot(attn_out[...], w_out[...])
    residual[...] = total
    normed_two[...] = (total * row_scale(total) * vectors[1:2]).astype(BF16)
    grads_step(2)
    for k in range(n_ctx // 2):
        spread_farther(k)
    for step in range(3, line_len):
        grads_step(step)
    for k in range(n_ctx // 2, n_ctx):
        spread_farther(k)
    for copy in on_near + on_farther + grads_pair + on_down[1:]:
        copy.wait_recv()
    for copy in sent:
        copy.wait_send()
    for copy in local:
        copy.wait()


def front(matrices, gate, up, hidden, tables, own_places, down, out_grad, collective_id, name):
    n_batch, n_ctx = lax.axis_size("batch"), lax.axis_size("ctx")
    line_len = n_ctx // 2
    rows = gate.shape[0]
    count, width = hidden.shape
    wide = width + 2 * KVW
    columns = (n_ctx, rows, 2 * lanes(gate.shape[1] // n_ctx))

    def shaped(dtype, *shape):
        return jax.ShapeDtypeStruct(shape, dtype)

    def room(*shape, dtype=BF16):
        return pltpu.VMEM(shape, dtype)

    return pl.pallas_call(
        functools.partial(front_kernel, line_len, 3),
        out_shape=(
            shaped(BF16, count, width),
            shaped(BF16, count, width),
            shaped(BF16, count, width),
            shaped(F32, count, width),
            shaped(BF16, count, width),
            shaped(F32, 1, width),
            shaped(F32, 1, width),
            shaped(F32, n_ctx, count),
            shaped(F32, n_ctx, count),
            shaped(BF16, n_ctx, count, 2 * KVW),
            shaped(BF16, width, wide + 128),
            shaped(BF16, width, width),
            *[shaped(BF16, *columns)] * 4,
            shaped(BF16, n_batch, *down.shape),
            shaped(BF16, n_ctx, count, width),
        ),
        in_specs=[IN_VMEM] * 14,
        out_specs=(IN_VMEM,) * 9 + (ANYWHERE,) * 9,
        scratch_shapes=[
            room(rows, wide + 128),
            room(width, wide + 128),
            room(width, width),
            room(*columns),
            room(count, 2 * KVW),
            room(n_ctx, count, 2 * KVW),
            room(n_ctx * count, count, dtype=F32),
            room(8, width, dtype=F32),
            room(1, 2 * KVW, dtype=F32),
            DMA((6,)),
            DMA((2, 2, line_len)),
            DMA((2, 2, line_len)),
            DMA((2, 2, n_ctx)),
            DMA((2, 2, 2 * n_ctx)),
            DMA((2, n_ctx)),
            DMA((2, n_ctx)),
            DMA((2, n_ctx)),
            DMA((2, n_ctx)),
            DMA((2, line_len)),
            DMA((2, line_len)),
            DMA((2, line_len)),
            DMA((2, line_len)),
            DMA((2, 3)),
        ],
        compiler_params=pltpu.CompilerParams(
            collective_id=collective_id, has_side_effects=True, vmem_limit_bytes=58 * 2**20
        ),
        cost_estimate=lasting(100),
        name=name,
    )(*matrices, gate, up, hidden, *tables, *own_places, down, out_grad)


def back_kernel(line_len, group, *refs):
    (
        query, key_value, key_pos, key_doc, own_pos, own_doc, attn_out, residual, gain_two, out_grad,
        d_normed, cosine, signed_sine, normed, hidden, gain_one, in_weights, out_weights, columns,
    ) = refs[:19]
    hidden_grad, o_out, q_out, kv_out, sums_out, columns_out = refs[19:25]
    w_out, w_in, branch, allowed, key_sum, value_sum, d_query, flipped, d_residual = refs[25:34]
    d_key_value, keys_pair, keys_line, keys_pass, sums_got, sums_mine = refs[34:40]
    grads = refs[40:43]
    core_in, chip_in, pair_in, line_in, chip_out, pair_out, line_out = [
        refs[43 + 3 * i : 46 + 3 * i] for i in range(7)
    ]
    (
        load_sems, column_sems, keys_pair_sems, keys_line_sems, sums_sems, core_sems, chip_sems,
        pair_sems, line_sems,
    ) = refs[64:]
    outs = o_out, q_out, kv_out
    b, c = lax.axis_index("batch"), lax.axis_index("ctx")
    n_ctx = 2 * line_len
    line, pair = c // 2, c % 2
    ahead = (b, 2 * lax.rem(line + 1, line_len) + pair)
    across, chip, core = (b, c ^ 1), (b ^ 2, c), (b ^ 1, c)
    others = [(b, lax.rem(c + k, n_ctx)) for k in range(1, n_ctx)]
    on_same_line = others[1::2]
    count, width = query.shape
    wide = group * HEAD_DIM
    rows = q_out.shape[0]
    greet([chip, core] + others)
    sent = []

    def send(source, target, sems, index, device):
        copy = remote(source, target, sems.at[(0, *index)], sems.at[(1, *index)], device)
        copy.start()
        sent.append(copy)
        return copy

    loads = [
        pltpu.make_async_copy(out_weights, w_out, load_sems.at[0]),
        pltpu.make_async_copy(in_weights.at[:, pl.ds(0, width + 2 * KVW)], w_in, load_sems.at[1]),
        pltpu.make_async_copy(columns.at[c], columns_out.at[c], load_sems.at[2]),
    ]
    for copy in loads:
        copy.start()
    on_columns = []

    def exchange_columns(first, last):
        for k in range(first, last):
            source = columns.at[others[k][1]]
            on_columns.append(send(source, columns_out.at[c], column_sems, (k,), others[k]))

    exchange_columns(0, n_ctx - 1)

    def to(step):
        return 2 * lax.rem(line - 1 - step + line_len, line_len)

    def place(index):
        return to(index // 2) + (1 - pair if index % 2 == 0 else pair)

    def block(row, index):
        at = (row * n_ctx + place(index)) * rows
        return pl.ds(pl.multiple_of(at, rows), rows)

    to_core, to_chip, to_pair, to_line = {}, {}, {}, {}

    def core_stage(p):
        for index in range(2 * n_ctx):
            row = b ^ 3 if index < n_ctx else b ^ 1
            source = grads[p].at[block(row, index % n_ctx)]
            to_core[p, index] = send(source, core_in[p].at[index], core_sems, (p, index), core)

    def chip_stage(p):
        for index in range(n_ctx):
            to_core[p, index].wait_recv()
            total = grads[p][block(b ^ 2, index)].astype(F32) + core_in[p][index].astype(F32)
            chip_out[p][index] = total.astype(BF16)
            to_chip[p, index] = send(
                chip_out[p].at[index], chip_in[p].at[index], chip_sems, (p, index), chip
            )

    def mine(p, index):
        to_core[p, n_ctx + index].wait_recv()
        to_chip[p, index].wait_recv()
        return (
            grads[p][block(b, index)].astype(F32)
            + core_in[p][n_ctx + index].astype(F32)
            + chip_in[p][index].astype(F32)
        )

    def pair_stage(p, step):
        pair_out[p][step] = mine(p, 2 * step).astype(BF16)
        to_pair[p, step] = send(
            pair_out[p].at[step], pair_in[p].at[step], pair_sems, (p, step), across
        )

    def line_stage(p, step):
        total = mine(p, 2 * step + 1)
        to_pair[p, step].wait_recv()
        total = total + pair_in[p][step].astype(F32)
        if step > 0:
            to_line[p, step - 1].wait_recv()
            total = total + line_in[p][step - 1].astype(F32)
        if step < line_len - 1:
            line_out[p][step] = total.astype(BF16)
            to_line[p, step] = send(
                line_out[p].at[step], line_in[p].at[step], line_sems, (p, step), ahead
            )
        else:
            outs[p][...] = total

    values, gradient = residual[...], d_normed[...]
    factor = row_scale(values)
    scaled = gradient * gain_two[...]
    sums_mine[...] = jnp.zeros_like(sums_mine)
    sums_mine[3:4] = jnp.sum(gradient * values * factor, axis=0, keepdims=True)
    total = out_grad[...].astype(F32) + (
        factor * scaled
        - values * (factor * factor * factor) * jnp.mean(scaled * values, axis=-1, keepdims=True)
    )
    d_residual[...] = total
    branch[...] = total.astype(BF16)
    for i in range(HEADS // group):
        part = slice(i * wide, (i + 1) * wide)
        grads[0][part] = contract_rows(attn_out[:, part], branch[...]).astype(BF16)
    core_stage(0)
    mark_allowed(key_pos, key_doc, own_pos, own_doc, allowed)
    flipped[...] = normed[...].astype(F32).T.astype(BF16)
    tables = cosine[...], signed_sine[...]

    def attention(i):
        part = slice(i * wide, (i + 1) * wide)
        head = i * group // GROUPS
        key_part = slice(head * HEAD_DIM, (head + 1) * HEAD_DIM)
        value_part = slice(KVW + head * HEAD_DIM, KVW + (head + 1) * HEAD_DIM)
        keys, values = key_value[:, key_part], key_value[:, value_part]
        d_attn = times_transposed(branch[...], w_out[part]).astype(BF16)
        head_grads, queries = stack_heads(d_attn, group), stack_heads(query[:, part], group)
        probs = probabilities(keys, queries, allowed, group)
        d_probs = times_transposed(values, head_grads)
        delta = jnp.sum(probs * d_probs, axis=0, keepdims=True)
        d_scores = (probs * (d_probs - delta)).astype(BF16)
        key_term = dot(d_scores, queries)
        value_term = dot(probs.astype(BF16), head_grads)
        first = i * group % GROUPS == 0
        key_sum[...] = key_term if first else key_sum[...] + key_term
        value_sum[...] = value_term if first else value_sum[...] + value_term
        result = contract_rows(keys, d_scores).T * INV_ROOT
        for k in range(group):
            turned = turn_head(result[k * count : (k + 1) * count], *tables, back=True)
            at = (i * group + k) * HEAD_DIM
            d_query[:, at : at + HEAD_DIM] = turned.astype(BF16)
        if (i + 1) * group % GROUPS == 0:
            shape = d_key_value.shape[:2] + (HEAD_DIM,)
            d_key_value[:, :, key_part] = (key_sum[...] * INV_ROOT).astype(BF16).reshape(shape)
            d_key_value[:, :, value_part] = value_sum[...].astype(BF16).reshape(shape)

    loads[0].wait()
    attention(0)
    chip_stage(0)
    for i in range(1, HEADS // group):
        attention(i)

    given, passed = [], []
    for step in range(line_len):
        source = d_key_value.at[to(step) + 1 - pair]
        given.append(send(source, keys_pair.at[step], keys_pair_sems, (step,), across))
    key_total = None

    def keys_stage(step):
        given[step].wait_recv()
        total = d_key_value[to(step) + pair].astype(F32) + keys_pair[step].astype(F32)
        if step > 0:
            passed[step - 1].wait_recv()
            total = total + keys_line[step - 1].astype(F32)
        if step < line_len - 1:
            keys_pass[step] = total.astype(BF16)
            passed.append(
                send(keys_pass.at[step], keys_line.at[step], keys_line_sems, (step,), ahead)
            )
        return total

    last = line_len - 1
    for step in range(line_len // 2):
        pair_stage(0, step)
    half = width // 2
    for i in range(2):
        part = slice(i * half, (i + 1) * half)
        grads[1][:, part] = dot(flipped[...], d_query[:, part]).astype(BF16)
        if i == 0:
            keys_stage(0)
    core_stage(1)
    loads[1].wait()
    d_one = times_transposed(d_query[...], w_in[:, :width])
    for step in range(1, line_len):
        key_total = keys_stage(step)
        if step == 1:
            chip_stage(1)
        if line_len // 2 + step - 1 < line_len:
            pair_stage(0, line_len // 2 + step - 1)
        if step < last:
            line_stage(0, step - 1)
    heads = [
        turn_head(key_total[:, i * HEAD_DIM : (i + 1) * HEAD_DIM], *tables, back=True)
        for i in range(KV_HEADS)
    ]
    d_lin = jnp.concatenate(heads + [key_total[:, KVW:]], axis=1).astype(BF16)
    grads[2][...] = dot(flipped[...], d_lin).astype(BF16)
    core_stage(2)
    line_stage(0, last - 1)
    d_one = d_one + times_transposed(d_lin, w_in[:, width:])
    sums_mine[1:2] = jnp.sum(d_query[...].astype(F32), axis=0, keepdims=True)
    sums_mine[2:3, : 2 * KVW] = jnp.sum(d_lin.astype(F32), axis=0, keepdims=True)
    values = hidden[...].astype(F32)
    factor = row_scale(values)
    scaled = d_one * gain_one[...]
    sums_mine[0:1] = jnp.sum(d_one * values * factor, axis=0, keepdims=True)

    def start_sums(index, device):
        copy = remote(
            sums_mine, sums_got.at[index], sums_sems.at[0, index], sums_sems.at[1, index], device
        )
        copy.start()
        return copy

    def add_sums(index, copy):
        copy.wait()
        sums_mine[...] += sums_got[index]

    by_core = start_sums(0, core)
    pair_stage(1, 0)
    line_stage(0, last)
    add_sums(0, by_core)
    by_chip = start_sums(1, chip)
    chip_stage(2)
    hidden_grad[...] = d_residual[...] + (
        factor * scaled
        - values * (factor * factor * factor) * jnp.mean(scaled * values, axis=-1, keepdims=True)
    )
    for step in range(1, line_len):
        pair_stage(1, step)
        line_stage(1, step - 1)
    add_sums(1, by_chip)
    by_pair = start_sums(2, across)
    pair_stage(2, 0)
    line_stage(1, last)
    for step in range(1, line_len):
        pair_stage(2, step)
        line_stage(2, step - 1)
        if step == 1:
            add_sums(2, by_pair)
            by_line = [start_sums(3 + k, device) for k, device in enumerate(on_same_line)]
    line_stage(2, last)
    total = sums_mine[...]
    for k, copy in enumerate(by_line):
        copy.wait()
        total = total + sums_got[3 + k]
    sums_out[...] = total
    for copy in on_columns:
        copy.wait_recv()
    for copy in sent:
        copy.wait_send()
    loads[2].wait()


def back(query, key_value, weights, places, attn_out, residual, gain_two, out_grad, d_normed, tables, normed, hidden, gain_one, columns, collective_id, name):
    n_ctx = columns.shape[0]
    line_len, rows = n_ctx // 2, columns.shape[1]
    count, width = query.shape
    keys = key_value.shape[0]
    widths = width, width, 2 * KVW

    def room(*shape, dtype=BF16):
        return pltpu.VMEM(shape, dtype)

    def rooms(size):
        return [room(size, rows, part) for part in widths]

    outs = [(count, width)] + [(rows, part) for part in widths] + [(8, width)]
    return pl.pallas_call(
        functools.partial(back_kernel, line_len, 3),
        out_shape=(
            *[jax.ShapeDtypeStruct(shape, F32) for shape in outs],
            jax.ShapeDtypeStruct(columns.shape, BF16),
        ),
        in_specs=[IN_VMEM] * 16 + [ANYWHERE] * 3,
        out_specs=(IN_VMEM,) * 5 + (ANYWHERE,),
        scratch_shapes=[
            room(width, width),
            room(width, width + 2 * KVW),
            room(count, width),
            room(keys, count, dtype=F32),
            room(keys, HEAD_DIM, dtype=F32),
            room(keys, HEAD_DIM, dtype=F32),
            room(count, width),
            room(width, count),
            room(count, width, dtype=F32),
            room(n_ctx, count, 2 * KVW),
            room(line_len, count, 2 * KVW),
            room(line_len - 1, count, 2 * KVW),
            room(line_len - 1, count, 2 * KVW),
            room(2 + line_len, 8, width, dtype=F32),
            room(8, width, dtype=F32),
            *[room(width, part) for part in widths],
            *rooms(2 * n_ctx),
            *rooms(n_ctx),
            *rooms(line_len),
            *rooms(line_len - 1),
            *rooms(n_ctx),
            *rooms(line_len),
            *rooms(line_len - 1),
            DMA((3,)),
            DMA((2, n_ctx)),
            DMA((2, line_len)),
            DMA((2, line_len)),
            DMA((2, 2 + line_len)),
            DMA((2, 3, 2 * n_ctx)),
            DMA((2, 3, n_ctx)),
            DMA((2, 3, line_len)),
            DMA((2, 3, line_len)),
        ],
        compiler_params=pltpu.CompilerParams(
            collective_id=collective_id, has_side_effects=True, vmem_limit_bytes=60 * 2**20
        ),
        cost_estimate=lasting(90),
        name=name,
    )(
        query, key_value, *places, attn_out, residual, gain_two, out_grad, d_normed, *tables, normed,
        hidden, gain_one, *weights, columns,
    )


def swap(values, bit):
    size = lax.axis_size("batch")
    return lax.ppermute(values, "batch", [(i, i ^ bit) for i in range(size)])


def by_batch(values, b, n_batch):
    step = values.shape[1] // n_batch
    blocks = [lax.dynamic_slice_in_dim(values, (b ^ k) * step, step, 1) for k in range(n_batch)]
    return jnp.concatenate(blocks, axis=1)


def batch_terms(terms):
    passed = swap((terms[2].astype(F32) + swap(terms[3], 1).astype(F32)).astype(BF16), 2)
    return [term.astype(F32) for term in (terms[0], swap(terms[1], 1), passed)]


def mlp_room(*sizes):
    return 2 * sum(math.prod(room.shape) for room in mlp_scratch(*sizes))


def mlp_in_steps(normed_two, w_gate_up, w_down, out_grad_all):
    n_batch, b = lax.axis_size("batch"), lax.axis_index("batch")
    normed_two = by_batch(normed_two, b, n_batch)
    w_gate_up = jnp.concatenate(w_gate_up, axis=0)
    half, width = w_gate_up.shape[1] // 2, normed_two.shape[1]
    own_ff = w_down.shape[0]
    w_down = jnp.pad(w_down, ((0, half - own_ff), (0, 0)))
    normed_two = gather_ctx(normed_two, 3, "gather_tokens").reshape(-1, width)
    gate_up = dot(normed_two, w_gate_up)
    gate_lin, up_lin = gate_up[:, :half], gate_up[:, half:]
    sigmoid_gate = jax.nn.sigmoid(gate_lin)
    mixed_rows = (gate_lin * sigmoid_gate * up_lin).astype(BF16)
    d_mixed = times_transposed(out_grad_all, w_down)
    d_gate = d_mixed * up_lin * sigmoid_gate * (1.0 + gate_lin * (1.0 - sigmoid_gate))
    d_up = d_mixed * (gate_lin * sigmoid_gate)
    d_gate_up = jnp.concatenate([d_gate.astype(BF16), d_up.astype(BF16)], axis=1)
    (d_normed_two,) = scatter_ctx(
        [times_transposed(d_gate_up, w_gate_up).astype(BF16)], 4, "scatter_tokens"
    )
    (ff_out,) = scatter_ctx([dot(mixed_rows, w_down).astype(BF16)], 8, "scatter_outputs")
    gate_up_grad = contract_rows(normed_two, d_gate_up).astype(BF16).reshape(n_batch, -1, 2 * half)
    down_grad = contract_rows(mixed_rows, out_grad_all).astype(BF16)[:own_ff]
    return (
        by_batch(d_normed_two, b, n_batch),
        ff_out,
        sum(
            batch_terms(
                [
                    lax.dynamic_index_in_dim(
                        down_grad.reshape(n_batch, -1, width), b ^ k, 0, keepdims=False
                    )
                    for k in range(n_batch)
                ]
            )
        ),
        sum(batch_terms(gate_up_grad)).astype(BF16),
    )


def vector_rows(vectors, rows, pieces):
    laid = [
        jnp.pad(v.reshape(pieces, 1, -1), ((0, 0), (0, 0), (0, 128 - v.shape[0] // pieces)))
        for v in vectors
    ]
    return jnp.pad(jnp.concatenate(laid, axis=1), ((0, 0), (0, rows - len(vectors)), (0, 0)))


def local(
    hidden_in,
    positions,
    doc_ids,
    attn_gain,
    q_weight,
    q_bias,
    k_weight,
    k_bias,
    v_weight,
    v_bias,
    o_weight,
    mlp_gain,
    gate_weight,
    up_weight,
    down_weight,
    out_grad,
):
    n_batch, n_ctx = lax.axis_size("batch"), lax.axis_size("ctx")
    n_all = n_batch * n_ctx
    count, width = hidden_in.shape
    hidden_ff = gate_weight.shape[1]

    b = lax.axis_index("batch")
    rows = q_weight.shape[0]
    small = (attn_gain, mlp_gain, q_bias, k_bias, v_bias)
    places = (positions // 64, positions % 64, doc_ids)
    small = vector_rows(small + tuple(row.astype(BF16) for row in places), rows, 1)[0]
    matrices = (q_weight, k_weight, v_weight, o_weight, small)
    cosine, sine_table = rope_tables(positions)
    half_lane = jnp.arange(HEAD_DIM) < HEAD_DIM // 2
    tables = cosine, jnp.where(half_lane[None], -sine_table, sine_table)
    own_places = positions.astype(F32)[None], doc_ids.astype(F32)[None]
    together = rows % 16 == 0
    if together:
        (
            normed_one, query, attn_out, residual, normed_two, gain_one, gain_two, key_pos, key_doc,
            key_value, *weights, packed, near, far, farther, w_down, out_grad_all,
        ) = front(
            matrices, gate_weight, up_weight, hidden_in, tables, own_places, down_weight, out_grad, 1,
            "front",
        )
        w_down = w_down.reshape(-1, width)
        half = packed.shape[2] // 2
        key_value = key_value.reshape(-1, 2 * KVW)
        w_gate_up = [columns.reshape(-1, 2 * half) for columns in (packed, near, far, farther)]
        places = (key_pos, key_doc, *own_places)
    else:
        w_down = lax.all_gather(down_weight, "batch", axis=0, tiled=True)
        out_grad_all = lax.all_gather(out_grad, "ctx", axis=0, tiled=True)
        attn_all, packed = spread(matrices, gate_weight, up_weight, 1, "spread_weights")
        half = packed.shape[2] // 2
        own_rows = packed.reshape(-1, 2 * half)
        near, far = swap(own_rows, 1), swap(own_rows, 2)
        small = attn_all[:, :, :8, attn_all.shape[3] - 128 :].astype(F32)
        gain_one, gain_two, b_query, b_key, b_value = (
            small[:, :, i, : part.shape[0]].reshape(-1)
            for i, part in enumerate((attn_gain, mlp_gain, q_bias, k_bias, v_bias))
        )
        places = lax.dynamic_index_in_dim(small, b, 0, keepdims=False)[:, 5:8, :count]
        key_pos, key_doc = places[:, 0] * 64 + places[:, 1], places[:, 2]
        attn_all = attn_all.reshape(width, -1)
        b_qkv = jnp.concatenate([b_query, b_key, b_value])
        gain_one, gain_two = gain_one[None], gain_two[None]

        normed_one, query, key_value = project(hidden_in, gain_one, attn_all, b_qkv[None], tables)
        key_value = gather_ctx(key_value, 2, "gather_keys").reshape(-1, 2 * KVW)
        far, key_value = lax.optimization_barrier((far, key_value))
        w_gate_up = (own_rows, near, far, swap(far, 1))
        places = (key_pos, key_doc, *own_places)
        attn_out, residual, normed_two = attend(
            query, key_value, attn_all, places, hidden_in, gain_two
        )

    fits = mlp_room(n_ctx, n_batch, count, width, w_down.shape[0]) < 56 * 2**20
    feed_forward = functools.partial(mlp, collective_id=3, name="mlp") if fits else mlp_in_steps
    d_normed_two, ff_out, down_grad, gate_up_grad = feed_forward(
        normed_two, w_gate_up, w_down, out_grad_all.reshape(-1, width)
    )
    hidden_out = (residual + ff_out).astype(BF16)

    columns = gate_up_grad.reshape(n_ctx, rows, 2 * half)
    if together:
        hidden_grad, o_grad, q_grad, kv_grad, sums, gate_up_grad = back(
            query, key_value, weights, places, attn_out, residual, gain_two, out_grad,
            d_normed_two, tables, normed_one, hidden_in, gain_one, columns, 7, "back"
        )
        k_grad, v_grad = kv_grad[:, :KVW], kv_grad[:, KVW:]
    else:
        d_query, d_key_value, o_grad, d_residual, gain_two_grad = attend_back(
            query, key_value, attn_all, places, attn_out, residual, gain_two, out_grad,
            d_normed_two, tables,
        )
        (d_key_value,) = scatter_ctx([d_key_value], 5, "scatter_keys")
        qkv_grad, hidden_grad, sums = project_back(
            d_query, d_key_value, attn_all, normed_one, hidden_in, gain_one, d_residual,
            gain_two_grad, tables,
        )
        grads = [grad.reshape(n_batch, n_ctx, rows, -1) for grad in (qkv_grad, o_grad)]
        qkv_grad, o_grad, sums, gate_up_grad = collect(grads, sums, columns, 6, "collect")
        q_grad, k_grad = qkv_grad[:, :width], qkv_grad[:, width : width + KVW]
        v_grad = qkv_grad[:, width + KVW :]
    gate_grad, up_grad = unpack(gate_up_grad, n_batch, hidden_ff)

    def own_part(row, first, total):
        size = total // n_all
        at = first + (b * n_ctx + lax.axis_index("ctx")) * size
        return lax.dynamic_slice(sums, (row, at), (1, size))[0]

    return (
        hidden_out,
        hidden_grad,
        own_part(0, 0, width),
        q_grad,
        own_part(1, 0, width),
        k_grad,
        own_part(2, 0, KVW),
        v_grad,
        own_part(2, KVW, KVW),
        o_grad,
        own_part(3, 0, width),
        gate_grad,
        up_grad,
        down_grad,
    )


def solution(mesh):
    matrix, vector = P(ALL, None), P(ALL)
    placed = (
        (matrix, vector, vector, vector, matrix, vector, matrix, vector)
        + (matrix, vector, matrix, vector, matrix, matrix, matrix, matrix)
    )
    results = (matrix, matrix) + (vector, matrix) * 4 + (vector, matrix, matrix, matrix)
    return jax.shard_map(local, mesh=mesh, in_specs=placed, out_specs=results, check_vma=False)
```

profile of v0, /device:TPU:0, one launch (start us, length us, event | category | flops | bytes accessed | tf_op | source)
XLA Modules:
  0.0 370.7 jit_solution(11031400013966107716)
XLA Ops:
  0.6 1.2 convert_bitcast_fusion.3
  1.9 1.2 convert_bitcast_fusion
  3.1 0.7 pad.21
  3.8 0.7 pad.22
  4.5 0.7 pad.23
  5.1 0.7 pad.24
  5.8 0.7 pad.25
  6.5 0.6 pad_bitcast_fusion.refs_4_
  7.1 0.1 broadcast_multiply_fusion
  7.2 1.0 negate_select_fusion
  8.2 130.8 %front.1 = (bf16[128,1536]{1,0:T(8,128)(2,1)}, bf16[128,1536]{1,0:T(8,128)(2,1)}, bf16[128,1536]{1,0:T(8,128)(2,1)}, f32[128,1536]{1,0:T(8,128)}, bf16[128,1536]...) custom-call(bf16[48,1536]{1,0:T(8,128)(2,1)} %refs_0_.1, ...), custom_call_target="tpu_custom_call" | custom-call | bytes 330000000 | tf_op jit(solution)/shard_map/front/pallas_call | solution.py:1455
  139.0 123.2 %mlp.1 = (f32[128,1536]{1,0:T(8,128)}, f32[128,1536]{1,0:T(8,128)}, f32[280,1536]{1,0:T(8,128)}, bf16[384,2304]{1,0:T(8,128)(2,1)}) custom-call(bf16[128,1536]{1,0:T(8,128)(2,1)} %get-tuple-element.45.own_rows, bf16[384,2304]{1,0:T(8,128)(2,1)} %bitcast.36, bf16[384,2304]{1,0:T(8,128)(2,1)} %bitcast.37, bf16[384,2304]{1,0:T(8,128)(2,1)} %bitcast.38, ...), custom_call_target="tpu_custom_call" | custom-call | bytes 330000000 | tf_op jit(solution)/shard_map/mlp/pallas_call | solution.py:1155
  262.2 0.0 copy-start.4
  262.2 96.8 %back.1 = (f32[128,1536]{1,0:T(8,128)}, f32[48,1536]{1,0:T(8,128)}, f32[48,1536]{1,0:T(8,128)}, f32[48,512]{1,0:T(8,128)}, f32[8,1536]{1,0:T(8,128)}, /*index=5*/bf16[8,48,2304]{2,1,0:T(8,128)(2,1)}) custom-call(bf16[128,1536]{1,0:T(8,128)(2,1)} %get-tuple-element.53.refs_0_, bf16[1024,512]{1,0:T(8,128)(2,1)} %bitcast.40, ...), custom_call_target="tpu_custom_call" | custom-call | bytes 297000000 | tf_op jit(solution)/shard_map/back/pallas_call | solution.py:1786
  359.0 1.5 copy-done
  360.4 2.3 unpack.1
  362.8 0.6 fusion.5
  363.4 1.3 fusion.2
  364.7 1.4 dynamic-slice_bitcast_fusion
  366.1 0.8 add_convert_fusion
  367.0 0.9 copy.34
  367.8 0.7 copy.35
  368.6 0.7 copy.36
  369.3 1.2 copy.37
  (17 shorter events, 0.1 us)
Async XLA Ops:
  262.2 103.9 %copy-start.4 = (f32[128,1536]{1,0:T(8,128)S(1)}, f32[128,1536]{1,0:T(8,128)}, u32[]{:S(2)}) copy-start(f32[128,1536]{1,0:T(8,128)} %get-tuple-element.52) | copy-start | bytes 2359300
  359.0 1.5 copy-start
  360.4 2.4 copy-start.7
  360.4 5.7 %copy-start.1 = (f32[128,1536]{1,0:T(8,128)S(1)}, f32[128,1536]{1,0:T(8,128)}, u32[]{:S(2)}) copy-start(f32[128,1536]{1,0:T(8,128)} %get-tuple-element.44.refs_7_) | copy-start | bytes 2359300
  360.4 6.5 %copy-start.3 = (f32[128,1536]{1,0:T(8,128)S(1)}, f32[128,1536]{1,0:T(8,128)}, u32[]{:S(2)}) copy-start(f32[128,1536]{1,0:T(8,128)} %get-tuple-element.104) | copy-start | bytes 2359300
  366.1 1.7 copy-start.6
  366.1 2.4 copy-start.5
  366.9 2.3 copy-start.2
where the time goes:
time: 378 us; the launch traced here: 371 us
  Pallas kernels  353 us (93%)
  local copies, waits for them, and re-layouts  12.2 us (3%)
  other arithmetic  4.39 us (1%)
    pallas_call x1, Pallas kernels, front(): pl.pallas_call(functools.partial(front_kernel, line_len, 3), out_shape=(s...  131 us
    pallas_call x1, Pallas kernels, mlp(): pl.pallas_call(functools.partial(mlp_kernel, line_len, tile), out_shape=(...  123 us
    pallas_call x1, Pallas kernels, back(): pl.pallas_call(functools.partial(back_kernel, line_len, 3), out_shape=(*[...  96.8 us

commit v1 on v0

--- a/solution.py
+++ b/solution.py
@@ -846,6 +846,49 @@
                 out[:, to : to + piece] = packed[i, :, at : at + piece].astype(F32)
 
 
+def finish_kernel(
+    n_batch, piece, packed, hidden_grad, o_grad, q_grad, kv_grad, residual, ff_rows, down_grad, sums,
+    gate, up, hidden_grad_out, o_out, q_out, k_out, v_out, hidden_out, down_out, own_sums,
+):
+    unpack_kernel(n_batch, piece, packed, gate, up)
+    hidden_grad_out[...] = hidden_grad[...]
+    o_out[...] = o_grad[...]
+    q_out[...] = q_grad[...]
+    k_out[...] = kv_grad[:, :KVW]
+    v_out[...] = kv_grad[:, KVW:]
+    hidden_out[...] = (residual[...] + ff_rows[...]).astype(BF16)
+    down_out[...] = down_grad[...]
+    n_ctx, rows, _ = packed.shape
+    width = sums.shape[1]
+    own = lax.axis_index("batch") * n_ctx + lax.axis_index("ctx")
+    small = KVW // (n_batch * n_ctx)
+    for row, first in ((0, own * rows), (1, own * small), (2, KVW + own * small)):
+        rolled = pltpu.roll(sums[...], lax.rem(width - first, width), 1)
+        own_sums[8 * row : 8 * row + 8] = rolled[:, :128]
+
+
+def finish(packed, hidden_grad, o_grad, q_grad, kv_grad, residual, ff_rows, down_grad, sums, n_batch, width):
+    n_ctx, rows, _ = packed.shape
+    wide = jax.ShapeDtypeStruct((rows, width), F32)
+    half = jax.ShapeDtypeStruct((rows, KVW), F32)
+
+    def like(array, dtype=F32):
+        return jax.ShapeDtypeStruct(array.shape, dtype)
+
+    return pl.pallas_call(
+        functools.partial(finish_kernel, n_batch, width // (n_batch * n_ctx)),
+        out_shape=(
+            wide, wide, like(hidden_grad), like(o_grad), like(q_grad), half, half,
+            like(residual, BF16), like(down_grad), jax.ShapeDtypeStruct((24, 128), F32),
+        ),
+        in_specs=[IN_VMEM] * 9,
+        out_specs=(IN_VMEM,) * 10,
+        compiler_params=pltpu.CompilerParams(vmem_limit_bytes=56 * 2**20),
+        cost_estimate=lasting(5),
+        name="finish",
+    )(packed, hidden_grad, o_grad, q_grad, kv_grad, residual, ff_rows, down_grad, sums)
+
+
 def unpack(packed, n_batch, width):
     n_ctx, rows, _ = packed.shape
     out = jax.ShapeDtypeStruct((rows, width), F32)
@@ -860,14 +903,14 @@
     )(packed)
 
 
-def mlp_kernel(line_len, tile, own_rows, *refs):
+def mlp_kernel(line_len, tile, span, own_rows, *refs):
     n_batch, n_ctx = 4, 2 * line_len
     weights, (down, grads_in) = refs[:n_batch], refs[n_batch : n_batch + 2]
     d_rows_out, ff_out, down_out, gate_up_out = refs[n_batch + 2 : n_batch + 6]
     (
         tokens, flipped, gate_up, down_in, grads, mixed, mixed_flipped, d_gate_up, d_parts, ff_parts,
-        d_pair, d_line, d_pass, ff_pair, ff_line, ff_pass, core_wide, chip_wide, down_terms,
-        core_down, chip_down, own, load_sems, store_sems,
+        d_pair, d_line, ff_pair, ff_line, core_wide, chip_wide, down_terms,
+        core_down, chip_down, own, lin, d_mixed_rows, load_sems, store_sems,
         line_sems, pair_sems, back_pair, back_line, batch_sems,
     ) = refs[n_batch + 6 :]
     b, c = lax.axis_index("batch"), lax.axis_index("ctx")
@@ -934,12 +977,15 @@
         block = tokens[pair_rows].reshape(2 * count, width)
         grad_block = grads[pair_rows].reshape(2 * count, width)
 
+        for low in range(0, 2 * half, span):
+            lin[:, low : low + span] = dot(block, gate_up[:, low : low + span])
+        d_mixed_rows[...] = times_transposed(grad_block, down_in[...])
+
         def columns(index, _):
             low = pl.multiple_of(index * tile, 128)
             high = pl.multiple_of(half + index * tile, 128)
-            gate_lin = dot(block, gate_up[:, pl.ds(low, tile)])
-            up_lin = dot(block, gate_up[:, pl.ds(high, tile)])
-            d_mixed = times_transposed(grad_block, down_in[pl.ds(low, tile)])
+            gate_lin, up_lin = lin[:, pl.ds(low, tile)], lin[:, pl.ds(high, tile)]
+            d_mixed = d_mixed_rows[:, pl.ds(low, tile)]
             sigmoid = 1.0 / (1.0 + jnp.exp(-gate_lin))
             silu = gate_lin * sigmoid
             product = silu * up_lin
@@ -951,31 +997,21 @@
             return 0
 
         lax.fori_loop(0, half // tile, columns, 0)
-
-        def features(index, _):
-            low = pl.multiple_of(index * depth, 128)
-            at_low = pl.ds(low, depth)
-            back = times_transposed(d_gate_up[rows], gate_up[at_low])
-            d_parts[pair_rows, :, at_low] = back.astype(BF16).reshape(2, count, depth)
-            return 0
-
-        lax.fori_loop(0, n_batch, features, 0)
-
-        def outputs(index, _):
-            low = pl.multiple_of(index * depth, 128)
-            at_low = pl.ds(low, depth)
-            out = dot(mixed[...], down_in[:, at_low])
-            ff_parts[pair_rows, :, at_low] = out.astype(BF16).reshape(2, count, depth)
-            flipped[at_low, rows] = (
-                tokens[pair_rows, :, at_low].reshape(2 * count, depth).astype(F32).T.astype(BF16)
+        for low in range(0, width, width // 2):
+            part = slice(low, low + width // 2)
+            back = times_transposed(d_gate_up[rows], gate_up[part])
+            d_parts[pair_rows, :, part] = back.astype(BF16).reshape(2, count, width // 2)
+        for low in range(0, width, width // 2):
+            part = slice(low, low + width // 2)
+            out = dot(mixed[...], down_in[:, part])
+            ff_parts[pair_rows, :, part] = out.astype(BF16).reshape(2, count, width // 2)
+            flipped[part, rows] = (
+                tokens[pair_rows, :, part].reshape(2 * count, width // 2).astype(F32).T.astype(BF16)
             )
-            return 0
-
-        lax.fori_loop(0, n_batch, outputs, 0)
 
     moves = (
-        (d_parts, d_pair, d_line, d_pass, d_rows_out),
-        (ff_parts, ff_pair, ff_line, ff_pass, ff_out),
+        (d_parts, d_pair, d_line, d_rows_out),
+        (ff_parts, ff_pair, ff_line, ff_out),
     )
     given = {}
 
@@ -1005,16 +1041,17 @@
     passed = {}
 
     def passing(index, which=0):
-        parts, pairs, lines, passes, out = moves[which]
+        parts, pairs, lines, out = moves[which]
+        place = at(index + 1) + pair
         given[index, which].wait_recv()
-        total = parts[at(index + 1) + pair].astype(F32) + pairs[index].astype(F32)
+        total = parts[place].astype(F32) + pairs[index].astype(F32)
         if index > 0:
             passed[index - 1, which].wait_recv()
             total = total + lines[index - 1].astype(F32)
         if index < line_len - 1:
-            passes[index] = total.astype(BF16)
+            parts[place] = total.astype(BF16)
             sems = back_line.at[0, which, index], back_line.at[1, which, index]
-            passed[index, which] = send(passes.at[index], lines.at[index], sems, ahead)
+            passed[index, which] = send(parts.at[place], lines.at[index], sems, ahead)
         elif which:
             out[...] = total
         else:
@@ -1030,13 +1067,8 @@
         return gate_up.at[pl.ds(k * depth, depth), pl.ds(side * half, half)]
 
     def weight_grad(k, side):
-        def columns(index, _):
-            at_low = pl.ds(pl.multiple_of(side * half + index * tile, 128), tile)
-            grad = dot(flipped[k * depth : (k + 1) * depth], d_gate_up[:, at_low])
-            gate_up[k * depth : (k + 1) * depth, at_low] = grad.astype(BF16)
-            return 0
-
-        lax.fori_loop(0, half // tile, columns, 0)
+        part = slice(k * depth, (k + 1) * depth), slice(side * half, (side + 1) * half)
+        gate_up[part] = dot(flipped[part[0]], d_gate_up[:, part[1]]).astype(BF16)
 
     def down_grads():
         for k in range(n_batch):
@@ -1136,13 +1168,15 @@
         room(tokens, 2 * half),
         room(n_ctx, count, width),
         room(n_ctx, count, width),
-        *[room(line_len, count, width), *[room(line_len - 1, count, width)] * 2] * 2,
+        *[room(line_len, count, width), room(line_len - 1, count, width)] * 2,
         room(2, 2, width // n_batch, half),
         room(2, width // n_batch, half),
         room(n_batch, piece, width),
         room(2, piece, width),
         room(piece, width),
         room(count, width),
+        pltpu.VMEM((2 * count, 2 * half), F32),
+        pltpu.VMEM((2 * count, half), F32),
     ]
 
 
@@ -1152,8 +1186,9 @@
     count, width = own.shape
     half = weights[0].shape[1] // 2
     tile = 384 if half % 384 == 0 else 128
+    span = 768 if 2 * half % 768 == 0 else tile
     return pl.pallas_call(
-        functools.partial(mlp_kernel, line_len, tile),
+        functools.partial(mlp_kernel, line_len, tile, span),
         out_shape=(
             jax.ShapeDtypeStruct((count, width), F32),
             jax.ShapeDtypeStruct((count, width), F32),
@@ -1173,7 +1208,7 @@
             DMA((2, 9)),
         ],
         compiler_params=pltpu.CompilerParams(
-            collective_id=collective_id, has_side_effects=True, vmem_limit_bytes=60 * 2**20
+            collective_id=collective_id, has_side_effects=True, vmem_limit_bytes=62 * 2**20
         ),
         cost_estimate=lasting(100),
         name=name,
@@ -1182,18 +1217,19 @@
 
 def front_kernel(line_len, group, *refs):
     (
-        q_weight, k_weight, v_weight, o_weight, small, gate, up, hidden, cosine, signed_sine,
-        own_pos, own_doc, down, out_grad,
-    ) = refs[:14]
+        q_weight, k_weight, v_weight, o_weight, gate, up, hidden, cosine, signed_sine, own_pos,
+        own_doc, down, out_grad,
+    ) = refs[:13]
+    own_vectors = refs[13:18]
     (
         normed_out, query, attn_out, residual, normed_two, gain_one, gain_two, key_pos, key_doc,
         key_value_out, w_in_out, w_out_out, columns_out, near, far, farther, down_out, grads_out,
-    ) = refs[14:32]
-    own_in, w_in, w_out, columns, key_own, key_value, allowed, vectors, bias = refs[32:41]
+    ) = refs[18:36]
+    own_in, w_in, w_out, columns, key_own, key_value, allowed, vectors, bias, small = refs[36:46]
     (
         load_sems, line_sems, first_sems, second_sems, core_sems, column_sems, near_sems, far_sems,
         farther_sems, keys_line_sems, keys_pair_sems, grads_line_sems, grads_pair_sems, down_sems,
-    ) = refs[41:]
+    ) = refs[46:]
     b, c = lax.axis_index("batch"), lax.axis_index("ctx")
     n_batch, n_ctx = 4, 2 * line_len
     line, pair = c // 2, c % 2
@@ -1207,7 +1243,14 @@
     for part in (q_weight, k_weight, v_weight):
         own_in[:, at : at + part.shape[1]] = part[...]
         at += part.shape[1]
-    own_in[:, at:] = small[...]
+    small[...] = jnp.zeros_like(small)
+    for row, vector in enumerate(own_vectors):
+        small[row : row + 1, : vector.shape[1]] = vector[...].astype(F32)
+    small[5:6] = jnp.right_shift(own_pos[...], 6).astype(F32)
+    small[6:7] = jnp.bitwise_and(own_pos[...], 63).astype(F32)
+    small[7:8] = own_doc[...].astype(F32)
+    own_in[:, at:] = jnp.zeros((rows, 128), BF16)
+    own_in[:8, at:] = small[...].astype(BF16)
     greet([chip, core] + others)
     sent, local = [], []
 
@@ -1354,6 +1397,8 @@
             exchange_columns(len(on_columns), len(on_columns) + 1)
     store(out_grad, grads_out.at[c])
     complete(0)
+    for k in range(3):
+        spread_columns(k)
 
     values = hidden[...].astype(F32)
     for d in range(n_batch * n_ctx):
@@ -1388,14 +1433,14 @@
             query[:, low : low + HEAD_DIM] = head.astype(BF16)
     store(w_in, w_in_out)
     mark_allowed(key_pos, key_doc, own_pos, own_doc, allowed)
-    spread_columns(0)
     for step in range(1, line_len):
         second_step(1, step - 1)
         keys_step(step)
+        spread_columns(len(on_near))
+    grads_step(0)
     for step in range(line_len):
         keys_pair[step].wait_recv()
     store(key_value, key_value_out)
-    grads_step(0)
 
     def attention(i):
         wide_part = group * HEAD_DIM
@@ -1411,23 +1456,20 @@
     steps = HEADS // group
     for i in range(steps):
         attention(i)
+        if i + 1 < line_len:
+            grads_step(i + 1)
         for index in range(line_len - 1 + i, n_ctx, steps):
             second_step(1, index)
-        for k in range(1 + 2 * i, min(3 + 2 * i, n_ctx)):
-            spread_columns(k)
-        if i == steps // 2:
-            grads_step(1)
+        if len(on_near) < n_ctx:
+            spread_columns(len(on_near))
     down_step(1)
     complete(1)
     store(w_out, w_out_out)
     total = hidden[...].astype(F32) + dot(attn_out[...], w_out[...])
     residual[...] = total
     normed_two[...] = (total * row_scale(total) * vectors[1:2]).astype(BF16)
-    grads_step(2)
     for k in range(n_ctx // 2):
         spread_farther(k)
-    for step in range(3, line_len):
-        grads_step(step)
     for k in range(n_ctx // 2, n_ctx):
         spread_farther(k)
     for copy in on_near + on_farther + grads_pair + on_down[1:]:
@@ -1438,7 +1480,7 @@
         copy.wait()
 
 
-def front(matrices, gate, up, hidden, tables, own_places, down, out_grad, collective_id, name):
+def front(matrices, gate, up, hidden, tables, own_places, down, out_grad, vectors, collective_id, name):
     n_batch, n_ctx = lax.axis_size("batch"), lax.axis_size("ctx")
     line_len = n_ctx // 2
     rows = gate.shape[0]
@@ -1471,7 +1513,7 @@
             shaped(BF16, n_batch, *down.shape),
             shaped(BF16, n_ctx, count, width),
         ),
-        in_specs=[IN_VMEM] * 14,
+        in_specs=[IN_VMEM] * 11 + [ANYWHERE] * 2 + [IN_VMEM] * 5,
         out_specs=(IN_VMEM,) * 9 + (ANYWHERE,) * 9,
         scratch_shapes=[
             room(rows, wide + 128),
@@ -1483,6 +1525,7 @@
             room(n_ctx * count, count, dtype=F32),
             room(8, width, dtype=F32),
             room(1, 2 * KVW, dtype=F32),
+            room(8, 128, dtype=F32),
             DMA((6,)),
             DMA((2, 2, line_len)),
             DMA((2, 2, line_len)),
@@ -1503,7 +1546,7 @@
         ),
         cost_estimate=lasting(100),
         name=name,
-    )(*matrices, gate, up, hidden, *tables, *own_places, down, out_grad)
+    )(*matrices, gate, up, hidden, *tables, *own_places, down, out_grad, *vectors)
 
 
 def back_kernel(line_len, group, *refs):
@@ -1853,7 +1896,8 @@
 
 
 def mlp_room(*sizes):
-    return 2 * sum(math.prod(room.shape) for room in mlp_scratch(*sizes))
+    rooms = mlp_scratch(*sizes)
+    return sum(math.prod(room.shape) * jnp.dtype(room.dtype).itemsize for room in rooms)
 
 
 def mlp_in_steps(normed_two, w_gate_up, w_down, out_grad_all):
@@ -1895,12 +1939,12 @@
     )
 
 
-def vector_rows(vectors, rows, pieces):
-    laid = [
-        jnp.pad(v.reshape(pieces, 1, -1), ((0, 0), (0, 0), (0, 128 - v.shape[0] // pieces)))
-        for v in vectors
-    ]
-    return jnp.pad(jnp.concatenate(laid, axis=1), ((0, 0), (0, rows - len(vectors)), (0, 0)))
+def vector_rows(vectors):
+    pieces = []
+    for vector in vectors:
+        pieces += [vector, jnp.zeros((128 - vector.shape[0],), vector.dtype)]
+    pieces.append(jnp.zeros((128 * (8 - len(vectors)),), vectors[0].dtype))
+    return jnp.concatenate(pieces).reshape(8, 128)
 
 
 def local(
@@ -1928,22 +1972,20 @@
 
     b = lax.axis_index("batch")
     rows = q_weight.shape[0]
-    small = (attn_gain, mlp_gain, q_bias, k_bias, v_bias)
-    places = (positions // 64, positions % 64, doc_ids)
-    small = vector_rows(small + tuple(row.astype(BF16) for row in places), rows, 1)[0]
-    matrices = (q_weight, k_weight, v_weight, o_weight, small)
+    vectors = (attn_gain, mlp_gain, q_bias, k_bias, v_bias)
+    weights = (q_weight, k_weight, v_weight, o_weight)
     cosine, sine_table = rope_tables(positions)
     half_lane = jnp.arange(HEAD_DIM) < HEAD_DIM // 2
     tables = cosine, jnp.where(half_lane[None], -sine_table, sine_table)
-    own_places = positions.astype(F32)[None], doc_ids.astype(F32)[None]
+    own_places = positions[None], doc_ids[None]
     together = rows % 16 == 0
     if together:
         (
             normed_one, query, attn_out, residual, normed_two, gain_one, gain_two, key_pos, key_doc,
             key_value, *weights, packed, near, far, farther, w_down, out_grad_all,
         ) = front(
-            matrices, gate_weight, up_weight, hidden_in, tables, own_places, down_weight, out_grad, 1,
-            "front",
+            weights, gate_weight, up_weight, hidden_in, tables, own_places, down_weight, out_grad,
+            [vector[None] for vector in vectors], 1, "front",
         )
         w_down = w_down.reshape(-1, width)
         half = packed.shape[2] // 2
@@ -1953,7 +1995,12 @@
     else:
         w_down = lax.all_gather(down_weight, "batch", axis=0, tiled=True)
         out_grad_all = lax.all_gather(out_grad, "ctx", axis=0, tiled=True)
-        attn_all, packed = spread(matrices, gate_weight, up_weight, 1, "spread_weights")
+        marks = (positions // 64, positions % 64, doc_ids)
+        small = vector_rows(vectors + tuple(mark.astype(BF16) for mark in marks))
+        small = jnp.pad(small, ((0, rows - 8), (0, 0)))
+        attn_all, packed = spread(
+            (*weights, small), gate_weight, up_weight, 1, "spread_weights"
+        )
         half = packed.shape[2] // 2
         own_rows = packed.reshape(-1, 2 * half)
         near, far = swap(own_rows, 1), swap(own_rows, 2)
@@ -1977,12 +2024,11 @@
             query, key_value, attn_all, places, hidden_in, gain_two
         )
 
-    fits = mlp_room(n_ctx, n_batch, count, width, w_down.shape[0]) < 56 * 2**20
+    fits = mlp_room(n_ctx, n_batch, count, width, w_down.shape[0]) < 60 * 2**20
     feed_forward = functools.partial(mlp, collective_id=3, name="mlp") if fits else mlp_in_steps
     d_normed_two, ff_out, down_grad, gate_up_grad = feed_forward(
         normed_two, w_gate_up, w_down, out_grad_all.reshape(-1, width)
     )
-    hidden_out = (residual + ff_out).astype(BF16)
 
     columns = gate_up_grad.reshape(n_ctx, rows, 2 * half)
     if together:
@@ -1990,7 +2036,14 @@
             query, key_value, weights, places, attn_out, residual, gain_two, out_grad,
             d_normed_two, tables, normed_one, hidden_in, gain_one, columns, 7, "back"
         )
-        k_grad, v_grad = kv_grad[:, :KVW], kv_grad[:, KVW:]
+        (
+            gate_grad, up_grad, hidden_grad, o_grad, q_grad, k_grad, v_grad, hidden_out, down_grad, sums,
+        ) = finish(
+            gate_up_grad, hidden_grad, o_grad, q_grad, kv_grad, residual, ff_out, down_grad, sums,
+            n_batch, hidden_ff,
+        )
+        gain_one_grad, q_bias_grad, gain_two_grad = (sums[i, :rows] for i in (0, 1, 3))
+        k_bias_grad, v_bias_grad = (sums[i, : KVW // n_all] for i in (10, 18))
     else:
         d_query, d_key_value, o_grad, d_residual, gain_two_grad = attend_back(
             query, key_value, attn_all, places, attn_out, residual, gain_two, out_grad,
@@ -2005,25 +2058,29 @@
         qkv_grad, o_grad, sums, gate_up_grad = collect(grads, sums, columns, 6, "collect")
         q_grad, k_grad = qkv_grad[:, :width], qkv_grad[:, width : width + KVW]
         v_grad = qkv_grad[:, width + KVW :]
-    gate_grad, up_grad = unpack(gate_up_grad, n_batch, hidden_ff)
-
-    def own_part(row, first, total):
-        size = total // n_all
-        at = first + (b * n_ctx + lax.axis_index("ctx")) * size
-        return lax.dynamic_slice(sums, (row, at), (1, size))[0]
-
+        gate_grad, up_grad = unpack(gate_up_grad, n_batch, hidden_ff)
+        hidden_out = (residual + ff_out).astype(BF16)
+
+        def own_part(row, first, total):
+            size = total // n_all
+            at = first + (b * n_ctx + lax.axis_index("ctx")) * size
+            return lax.dynamic_slice(sums, (row, at), (1, size))[0]
+
+        gain_one_grad, q_bias_grad = own_part(0, 0, width), own_part(1, 0, width)
+        k_bias_grad, v_bias_grad = own_part(2, 0, KVW), own_part(2, KVW, KVW)
+        gain_two_grad = own_part(3, 0, width)
     return (
         hidden_out,
         hidden_grad,
-        own_part(0, 0, width),
+        gain_one_grad,
         q_grad,
-        own_part(1, 0, width),
+        q_bias_grad,
         k_grad,
-        own_part(2, 0, KVW),
+        k_bias_grad,
         v_grad,
-        own_part(2, KVW, KVW),
+        v_bias_grad,
         o_grad,
-        own_part(3, 0, width),
+        gain_two_grad,
         gate_grad,
         up_grad,
         down_grad,

time: 378 us -> 361 us (0.955)
  the two profiles are of different devices: /device:TPU:0 before, /device:TPU:10 now
where the time goes in v1:
time: 361 us; the launch traced here: 354 us
  Pallas kernels  349 us (97%)
    pallas_call x1, Pallas kernels, front(): pl.pallas_call(functools.partial(front_kernel, line_len, 3), out_shape=(s...  127 us
    pallas_call x1, Pallas kernels, mlp(): pl.pallas_call(functools.partial(mlp_kernel, line_len, tile, span), out_s...  117 us
    pallas_call x1, Pallas kernels, back(): pl.pallas_call(functools.partial(back_kernel, line_len, 3), out_shape=(*[...  98 us

profile of v1, /device:TPU:10, one launch (start us, length us, event | category | flops | bytes accessed | tf_op | source)
XLA Modules:
  0.0 354.0 jit_solution(7716441478875893814)
XLA Ops:
  0.6 0.7 convert_element_type.3
  1.3 0.1 broadcast_multiply_fusion
  1.4 1.0 negate_select_fusion
  2.4 126.8 %front.1 = (bf16[128,1536]{1,0:T(8,128)(2,1)}, bf16[128,1536]{1,0:T(8,128)(2,1)}, bf16[128,1536]{1,0:T(8,128)(2,1)}, f32[128,1536]{1,0:T(8,128)}, bf16[128,1536]...) custom-call(bf16[48,1536]{1,0:T(8,128)(2,1)} %refs_0_.1, ...), custom_call_target="tpu_custom_call" | custom-call | bytes 330000000 | tf_op jit(solution)/shard_map/front/pallas_call | solution.py:1497
  129.2 117.4 %mlp.1 = (f32[128,1536]{1,0:T(8,128)}, f32[128,1536]{1,0:T(8,128)}, f32[280,1536]{1,0:T(8,128)}, bf16[384,2304]{1,0:T(8,128)(2,1)}) custom-call(bf16[128,1536]{1,0:T(8,128)(2,1)} %get-tuple-element.59.own_rows, bf16[384,2304]{1,0:T(8,128)(2,1)} %bitcast.26, bf16[384,2304]{1,0:T(8,128)(2,1)} %bitcast.27, bf16[384,2304]{1,0:T(8,128)(2,1)} %bitcast.28, ...), custom_call_target="tpu_custom_call" | custom-call | bytes 330000000 | tf_op jit(solution)/shard_map/mlp/pallas_call | solution.py:1190
  246.6 98.0 %back.1 = (f32[128,1536]{1,0:T(8,128)}, f32[48,1536]{1,0:T(8,128)}, f32[48,1536]{1,0:T(8,128)}, f32[48,512]{1,0:T(8,128)}, f32[8,1536]{1,0:T(8,128)}, /*index=5*/bf16[8,48,2304]{2,1,0:T(8,128)(2,1)}) custom-call(bf16[128,1536]{1,0:T(8,128)(2,1)} %get-tuple-element.52.refs_0_, bf16[1024,512]{1,0:T(8,128)(2,1)} %bitcast.30, ...), custom_call_target="tpu_custom_call" | custom-call | bytes 297000000 | tf_op jit(solution)/shard_map/back/pallas_call | solution.py:1829
  344.6 6.5 %finish.1 = (f32[48,8960]{1,0:T(8,128)}, f32[48,8960]{1,0:T(8,128)}, f32[128,1536]{1,0:T(8,128)}, f32[48,1536]{1,0:T(8,128)}, f32[48,1536]{1,0:T(8,128)}, /*inde...) custom-call(bf16[8,48,2304]{2,1,0:T(8,128)(2,1)} %get-tuple-element., ...), custom_call_target="tpu_custom_call" | custom-call | bytes 16500000 | tf_op jit(solution)/shard_map/finish/pallas_call | solution.py:878
  351.1 1.2 slice_bitcast_fusion.1
  352.3 1.3 slice_bitcast_fusion
  (2 shorter events, 0.0 us)

commit v2 on v1

--- a/solution.py
+++ b/solution.py
@@ -1742,9 +1742,9 @@
     loads[1].wait()
     d_one = times_transposed(d_query[...], w_in[:, :width])
     for step in range(1, line_len):
-        key_total = keys_stage(step)
         if step == 1:
             chip_stage(1)
+        key_total = keys_stage(step)
         if line_len // 2 + step - 1 < line_len:
             pair_stage(0, line_len // 2 + step - 1)
         if step < last:

time: 361 us -> 361 us (level)
  no operation moved by 1% of the time
where the time goes in v2:
time: 361 us; the launch traced here: 354 us
  Pallas kernels  349 us (97%)
    pallas_call x1, Pallas kernels, front(): pl.pallas_call(functools.partial(front_kernel, line_len, 3), out_shape=(s...  127 us
    pallas_call x1, Pallas kernels, mlp(): pl.pallas_call(functools.partial(mlp_kernel, line_len, tile, span), out_s...  117 us
    pallas_call x1, Pallas kernels, back(): pl.pallas_call(functools.partial(back_kernel, line_len, 3), out_shape=(*[...  98.1 us

profile of v2, /device:TPU:10, one launch (start us, length us, event | category | flops | bytes accessed | tf_op | source)
XLA Modules:
  0.0 354.2 jit_solution(9433319234304627951)
XLA Ops:
  0.6 0.7 convert_element_type.3
  1.3 0.1 broadcast_multiply_fusion
  1.4 1.0 negate_select_fusion
  2.4 126.8 %front.1 = (bf16[128,1536]{1,0:T(8,128)(2,1)}, bf16[128,1536]{1,0:T(8,128)(2,1)}, bf16[128,1536]{1,0:T(8,128)(2,1)}, f32[128,1536]{1,0:T(8,128)}, bf16[128,1536]...) custom-call(bf16[48,1536]{1,0:T(8,128)(2,1)} %refs_0_.1, ...), custom_call_target="tpu_custom_call" | custom-call | bytes 330000000 | tf_op jit(solution)/shard_map/front/pallas_call | solution.py:1497
  129.2 117.4 %mlp.1 = (f32[128,1536]{1,0:T(8,128)}, f32[128,1536]{1,0:T(8,128)}, f32[280,1536]{1,0:T(8,128)}, bf16[384,2304]{1,0:T(8,128)(2,1)}) custom-call(bf16[128,1536]{1,0:T(8,128)(2,1)} %get-tuple-element.59.own_rows, bf16[384,2304]{1,0:T(8,128)(2,1)} %bitcast.26, bf16[384,2304]{1,0:T(8,128)(2,1)} %bitcast.27, bf16[384,2304]{1,0:T(8,128)(2,1)} %bitcast.28, ...), custom_call_target="tpu_custom_call" | custom-call | bytes 330000000 | tf_op jit(solution)/shard_map/mlp/pallas_call | solution.py:1190
  246.6 98.1 %back.1 = (f32[128,1536]{1,0:T(8,128)}, f32[48,1536]{1,0:T(8,128)}, f32[48,1536]{1,0:T(8,128)}, f32[48,512]{1,0:T(8,128)}, f32[8,1536]{1,0:T(8,128)}, /*index=5*/bf16[8,48,2304]{2,1,0:T(8,128)(2,1)}) custom-call(bf16[128,1536]{1,0:T(8,128)(2,1)} %get-tuple-element.52.refs_0_, bf16[1024,512]{1,0:T(8,128)(2,1)} %bitcast.30, ...), custom_call_target="tpu_custom_call" | custom-call | bytes 297000000 | tf_op jit(solution)/shard_map/back/pallas_call | solution.py:1829
  344.7 6.5 %finish.1 = (f32[48,8960]{1,0:T(8,128)}, f32[48,8960]{1,0:T(8,128)}, f32[128,1536]{1,0:T(8,128)}, f32[48,1536]{1,0:T(8,128)}, f32[48,1536]{1,0:T(8,128)}, /*inde...) custom-call(bf16[8,48,2304]{2,1,0:T(8,128)(2,1)} %get-tuple-element., ...), custom_call_target="tpu_custom_call" | custom-call | bytes 16500000 | tf_op jit(solution)/shard_map/finish/pallas_call | solution.py:878
  351.2 1.2 slice_bitcast_fusion.1
  352.4 1.3 slice_bitcast_fusion
  (2 shorter events, 0.0 us)
